TPU v7x, 32 devices: a whole 2x2x4 slice. The times are simulated.
32 devices in a mesh: row: 4 (over y, core), col: 8 (over z, x).
Axes of the slice: x: 2, y: 2, z: 4, core: 2. Of those that a mesh axis runs over, the one named last changes fastest.
Arguments:
- query_matrix: bfloat16 [32, 128, 768], P('row', 'col'), may hold values from -6 to 16.133757
- key_matrix: bfloat16 [32, 128, 768], P('row', 'col'), may hold values from -6 to 6
- value_matrix: bfloat16 [32, 128, 768], P('row', 'col'), may hold values from -6 to 6
- tissue: int32 [32, 128], replicated, may hold values 0 or 1
- dilation_levels: int32 [16], replicated, may hold values from 0 to 2
- segment_levels: int32 [16], replicated, may hold values from 0 to 2
- output_matrix: bfloat16 [768, 768], replicated, may hold values from -0.21875 to 0.21875
Outputs:
- encoded: bfloat16 [32, 128, 768], P('row', 'col')
Inputs may be any that keep to these rules, and one draw needn't show every extreme that they name: 1 marks a tissue tile, 0 background. Head h uses the dilation 8 * 2^dilation_levels[h]. Head h uses segments of 128 / 2^segment_levels[h] tiles of a grid row.
All inputs are finite; a program needn't handle non-finite values.
Results may differ from a plain program's by a relative error of at most 0.0055.
Values may be sent and summed in bfloat16 or wider, within the bound.
A program may use at most 64 MiB of HBM per device.

v0:
```python
import math

import jax
import jax.numpy as jnp
import numpy as np
from jax import lax
from jax.sharding import PartitionSpec as P

HEAD_COUNT = 16
R = 8
DILATION_MIN = 8


NEG_FILL = -1e30


def padded_2(x, sides, width):
    for axis, dim in sides:
        peers, length = (lax.axis_size(axis), x.shape[dim])
        up = [(i, (i + 1) % peers) for i in range(peers - 1)]
        down = [(j, i) for i, j in up]
        last = lax.slice_in_dim(x, length - width, length, axis=dim)
        first = lax.slice_in_dim(x, 0, width, axis=dim)
        before = lax.ppermute(last, axis, up)
        after = lax.ppermute(first, axis, down)
        x = jnp.concatenate([before, x, after], axis=dim)
    return x


def window_static(device_rows, device_columns):
    region_rows = np.arange(device_rows + 2 * R) - R
    query_rows = np.arange(device_rows)
    region_cols = np.arange(device_columns + 2 * R) - R
    query_cols = np.arange(device_columns)
    near_rows = np.abs(region_rows[None, :] - query_rows[:, None]) <= R
    near_cols = np.abs(region_cols[None, :] - query_cols[:, None]) <= R
    same_rows = region_rows[None, :] == query_rows[:, None]
    same_cols = region_cols[None, :] == query_cols[:, None]
    near_both = near_rows[:, None, :, None] & near_cols[None, :, None, :]
    self_both = same_rows[:, None, :, None] & same_cols[None, :, None, :]
    return (near_both, self_both)


def window_part(queries, key_region, value_region, permitted_mask, group_size):
    head_dimension = queries.shape[-1] // HEAD_COUNT
    scale = 1.0 / math.sqrt(head_dimension)
    numerators, maxima, totals = ([], [], [])
    for head_first in range(0, HEAD_COUNT, group_size):
        lower = head_first * head_dimension
        upper = (head_first + group_size) * head_dimension
        query_grp = queries[:, lower:upper].reshape(queries.shape[0], group_size, head_dimension)
        key_grp = key_region[:, lower:upper].reshape(
            key_region.shape[0], group_size, head_dimension
        )
        value_grp = value_region[:, lower:upper].reshape(
            value_region.shape[0], group_size, head_dimension
        )
        scores = (
            jnp.einsum("qhd,khd->hqk", query_grp, key_grp, preferred_element_type=jnp.float32)
            * scale
        )
        scores = jnp.where(permitted_mask[None], scores, NEG_FILL)
        highest = jnp.max(scores, axis=-1)
        exp_terms = jnp.exp(scores - highest[..., None])
        totals.append(jnp.sum(exp_terms, axis=-1))
        numerators.append(
            jnp.einsum(
                "hqk,khd->qhd",
                exp_terms.astype(jnp.bfloat16),
                value_grp,
                preferred_element_type=jnp.float32,
            )
        )
        maxima.append(highest)
    return (
        jnp.concatenate(numerators, axis=1),
        jnp.concatenate(maxima, axis=0).T,
        jnp.concatenate(totals, axis=0).T,
    )


def dilation_valid_mask(
    tissue,
    row_indices,
    head_indices,
    column_indices,
    dilation_levels,
    segment_levels,
    selected_count,
    column_total,
):
    key_columns = (
        jnp.arange(selected_count, dtype=jnp.int32)[None, :] * DILATION_MIN
        + (head_indices % DILATION_MIN)[:, None]
    )
    tissue_keys = tissue[row_indices[:, None], key_columns]
    dilation_stride = jnp.left_shift(jnp.int32(DILATION_MIN), dilation_levels[head_indices])
    segment = jnp.right_shift(jnp.int32(column_total), segment_levels[head_indices])
    phase_ok = key_columns % dilation_stride[:, None] == (head_indices % dilation_stride)[:, None]
    key_seg = key_columns // segment[:, None]
    query_seg = column_indices[None, :] // segment[:, None]
    same_seg = key_seg[:, None, :] == query_seg[:, :, None]
    return same_seg & ((tissue_keys == 1) & phase_ok)[:, None, :]


def dilation_partial(queries, keys_sel, values_sel, permitted_mask):
    scale = 1.0 / math.sqrt(queries.shape[-1])
    scores = (
        jnp.einsum("icw,isw->ics", queries, keys_sel, preferred_element_type=jnp.float32) * scale
    )
    scores = jnp.where(permitted_mask, scores, NEG_FILL)
    highest = jnp.max(scores, axis=-1)
    exp_terms = jnp.where(permitted_mask, jnp.exp(scores - highest[..., None]), 0.0)
    totals = jnp.sum(exp_terms, axis=-1)
    softmax_numer = jnp.einsum(
        "ics,isw->icw",
        exp_terms.astype(jnp.bfloat16),
        values_sel,
        preferred_element_type=jnp.float32,
    )
    return (softmax_numer, highest, totals)


def merge_partials(
    neighbour_numer, neighbour_max, neighbour_sum, dilation_numer, dilation_score_max, dilation_sum
):
    running_maximum = jnp.maximum(neighbour_max, dilation_score_max)
    neighbour_rescale = jnp.exp(neighbour_max - running_maximum)
    dilation_rescale = jnp.exp(dilation_score_max - running_maximum)
    softmax_numer = (
        neighbour_rescale[..., None] * neighbour_numer
        + dilation_rescale[..., None] * dilation_numer
    )
    softmax_denom = neighbour_rescale * neighbour_sum + dilation_rescale * dilation_sum
    return softmax_numer / softmax_denom[..., None]


def per_device(
    query_matrix, key_matrix, value_matrix, tissue, dilation_levels, segment_levels, output_matrix
):
    device_rows, device_columns, model_width = query_matrix.shape
    head_dimension = model_width // HEAD_COUNT
    col_count = lax.axis_size("col")
    column_total = device_columns * col_count
    selected_count = column_total // DILATION_MIN
    local_selection = device_columns // DILATION_MIN
    row_offset = lax.axis_index("row") * device_rows
    column_offset = lax.axis_index("col") * device_columns
    packed = jnp.concatenate([key_matrix, value_matrix], axis=-1)
    padded = padded_2(packed, (("row", 0), ("col", 1)), R)
    key_region = padded[:, :, :model_width].reshape(-1, model_width)
    value_region = padded[:, :, model_width:].reshape(-1, model_width)
    tissue_pad = jnp.pad(tissue, R)
    tissue_reg = lax.dynamic_slice(
        tissue_pad, (row_offset, column_offset), (device_rows + 2 * R, device_columns + 2 * R)
    )
    near_both, self_both = window_static(device_rows, device_columns)
    permitted_mask = jnp.asarray(near_both) & (tissue_reg[None, None] == 1) | jnp.asarray(self_both)
    permitted_mask = permitted_mask.reshape(device_rows * device_columns, -1)
    neighbour_numer, neighbour_max, neighbour_sum = window_part(
        query_matrix.reshape(-1, model_width), key_region, value_region, permitted_mask, 2
    )
    phase_table = np.arange(HEAD_COUNT)[None, :] % DILATION_MIN == np.arange(DILATION_MIN)[:, None]
    phase_table = jnp.asarray(phase_table)[None, None, :, :, None]
    key_phases = key_matrix.reshape(
        device_rows, local_selection, DILATION_MIN, HEAD_COUNT, head_dimension
    )
    value_phases = value_matrix.reshape(
        device_rows, local_selection, DILATION_MIN, HEAD_COUNT, head_dimension
    )
    zero_entry = jnp.zeros((), jnp.bfloat16)
    key_selected = jnp.sum(
        jnp.where(phase_table, key_phases, zero_entry), axis=2, dtype=jnp.bfloat16
    ).reshape(device_rows, local_selection, model_width)
    value_selected = jnp.sum(
        jnp.where(phase_table, value_phases, zero_entry), axis=2, dtype=jnp.bfloat16
    ).reshape(device_rows, local_selection, model_width)
    token_count = device_rows * HEAD_COUNT
    per_target = token_count // col_count
    query_tokens = query_matrix.reshape(
        device_rows, device_columns, HEAD_COUNT, head_dimension
    ).transpose(0, 2, 1, 3)
    q_send = query_tokens.reshape(col_count, per_target, device_columns, head_dimension)
    k_send = (
        key_selected.reshape(device_rows, local_selection, HEAD_COUNT, head_dimension)
        .transpose(0, 2, 1, 3)
        .reshape(col_count, per_target, local_selection, head_dimension)
    )
    v_send = (
        value_selected.reshape(device_rows, local_selection, HEAD_COUNT, head_dimension)
        .transpose(0, 2, 1, 3)
        .reshape(col_count, per_target, local_selection, head_dimension)
    )
    id_send = jnp.arange(token_count, dtype=jnp.int32).reshape(col_count, per_target, 1)
    query_got = lax.all_to_all(q_send, "col", split_axis=0, concat_axis=2, tiled=True)
    key_got = lax.all_to_all(k_send, "col", split_axis=0, concat_axis=2, tiled=True)
    value_got = lax.all_to_all(v_send, "col", split_axis=0, concat_axis=2, tiled=True)
    id_got = lax.all_to_all(id_send, "col", split_axis=0, concat_axis=2, tiled=True)
    item_ids = id_got[0, :, 0]
    all_cols = jnp.arange(column_total, dtype=jnp.int32)
    got_allowed = dilation_valid_mask(
        tissue,
        row_offset + item_ids // HEAD_COUNT,
        item_ids % HEAD_COUNT,
        all_cols,
        dilation_levels,
        segment_levels,
        selected_count,
        column_total,
    )
    softmax_numer, highest, totals = dilation_partial(
        query_got[0], key_got[0], value_got[0], got_allowed
    )
    token_numer = lax.all_to_all(
        softmax_numer[None], "col", split_axis=2, concat_axis=0, tiled=True
    )
    token_max = lax.all_to_all(highest[None], "col", split_axis=2, concat_axis=0, tiled=True)
    token_sum = lax.all_to_all(totals[None], "col", split_axis=2, concat_axis=0, tiled=True)
    dilation_numer = (
        token_numer.reshape(device_rows, HEAD_COUNT, device_columns, head_dimension)
        .transpose(0, 2, 1, 3)
        .reshape(-1, HEAD_COUNT, head_dimension)
    )
    dilation_score_max = (
        token_max.reshape(device_rows, HEAD_COUNT, device_columns)
        .transpose(0, 2, 1)
        .reshape(-1, HEAD_COUNT)
    )
    dilation_sum = (
        token_sum.reshape(device_rows, HEAD_COUNT, device_columns)
        .transpose(0, 2, 1)
        .reshape(-1, HEAD_COUNT)
    )
    attended = (
        merge_partials(
            neighbour_numer,
            neighbour_max,
            neighbour_sum,
            dilation_numer,
            dilation_score_max,
            dilation_sum,
        )
        .reshape(-1, model_width)
        .astype(jnp.bfloat16)
    )
    encoded = jnp.dot(attended, output_matrix, preferred_element_type=jnp.float32).astype(
        jnp.bfloat16
    )
    return encoded.reshape(device_rows, device_columns, model_width)


def solution(mesh):
    in_specs = (
        P("row", "col", None),
        P("row", "col", None),
        P("row", "col", None),
        P(),
        P(),
        P(),
        P(),
    )
    out_specs = P("row", "col", None)
    return jax.shard_map(
        per_device, mesh=mesh, in_specs=in_specs, out_specs=out_specs, check_vma=False
    )
```

profile of v0, /device:TPU:0, one launch (start us, length us, event | category | flops | bytes accessed | tf_op | source)
XLA Modules:
  0.0 140.0 jit_solution(15998028674021231577)
XLA Ops:
  3.3 3.1 %collective-permute-start = (bf16[8,16,1536]{2,1,0:T(8,128)(2,1)S(1)}, bf16[8,16,1536]{2,1,0:T(8,128)(2,1)S(1)}, u32[]{:S(2)}, u32[]{:S(2)}) collective-permute-start(bf16[8,16,1536]{2,1,0:T(8,128)(2,1)S(1)} %constant_dynamic-update-slice_fusion), channel_id=1, source_target_pairs={{0,8},{8,16},{16,24},{1,9},{9,17},{17,25},{2,10},{10,18},{18,26},{... | collective-permute-start | bytes 1179656 | tf_op jit(solution)/shard_map/ppermute | solution.py:24
  7.0 7.3 %all-to-all-start = ((s32[8,16,1]{1,2,0:T(1,128)}), s32[8,16,1]{1,2,0:T(1,128)S(1)}, u32[]{:S(2)}, u32[]{:S(2)}) async-start(s32[8,16,1]{1,2,0:T(1,128)} %multiply_add_fusion), calls=%async_computation | async-start | bytes 8192 | tf_op jit(solution)/shard_map/all_to_all | solution.py:198
  14.2 1.5 %reshape.598 = bf16[8,2,8,16,48]{4,3,2,1,0:T(8,128)(2,1)S(1)} reshape(bf16[8,16,768]{2,1,0:T(8,128)(2,1)} %param.11) | data formatting | bytes 393216 | tf_op jit(solution)/shard_map/reshape | solution.py:165
  15.8 1.5 %reshape.610 = bf16[8,2,8,16,48]{4,3,2,1,0:T(8,128)(2,1)S(1)} reshape(bf16[8,16,768]{2,1,0:T(8,128)(2,1)} %param.12) | data formatting | bytes 393216 | tf_op jit(solution)/shard_map/reshape | solution.py:168
  18.1 2.2 %and_or_fusion = pred[8,16,24,32]{3,2,1,0:T(8,128)(4,1)} fusion(pred[8,16,24,32]{3,2,1,0:T(8,128)(4,1)} %constant.104.clone, pred[8,16,24,32]{3,2,1,0:T(8,128)(4,1)} %constant.103.clone, pred[24,32]{1,0:T(8,128)(4,1)S(1)} %fusion.72), kind=kLoop, calls=%fused_computation.4 | loop fusion | flops 196608 | bytes 295680 | tf_op jit(solution)/shard_map/or | solution.py:158
  21.3 1.5 %reshape.599 = bf16[8,16,16,48]{3,2,1,0:T(8,128)(2,1)S(1)} reshape(bf16[8,16,768]{2,1,0:T(8,128)(2,1)} %param.10) | data formatting | bytes 393216 | tf_op jit(solution)/shard_map/reshape | solution.py:180
  26.8 6.0 %all-to-all-start.1 = ((bf16[8,2,768]{2,1,0:T(2,128)(2,1)}), bf16[8,2,768]{2,1,0:T(2,128)(2,1)S(1)}, u32[]{:S(2)}, u32[]{:S(2)}) async-start(bf16[8,2,768]{2,1,0:T(2,128)(2,1)} %reshape.644), calls=%async_computation.1 | async-start | bytes 49152 | tf_op jit(solution)/shard_map/all_to_all | solution.py:196
  34.5 1.9 %gather_fusion.1 = s32[256]{0:T(256)S(1)} fusion(s32[32,128]{1,0:T(8,128)S(1)} %copy-done.1, s32[256]{0:T(256)S(1)} %reshape.622), kind=kCustom, calls=%fused_computation.1 | custom fusion | bytes 4096 | tf_op jit(solution)/shard_map/gather | solution.py:96
  36.7 2.7 %all-to-all-done.1 = bf16[8,2,768]{2,1,0:T(2,128)(2,1)S(1)} async-done(((bf16[8,2,768]{2,1,0:T(2,128)(2,1)}), bf16[8,2,768]{2,1,0:T(2,128)(2,1)S(1)}, u32[]{:S(2)}, u32[]{:S(2)}) %all-to-all-start.1) | async-done | bytes 24608 | tf_op jit(solution)/shard_map/all_to_all | solution.py:196
  39.4 3.4 %all-to-all-start.2 = ((bf16[8,2,6144]{2,1,0:T(2,128)(2,1)}), bf16[8,2,6144]{2,1,0:T(2,128)(2,1)S(1)}, u32[]{:S(2)}, u32[]{:S(2)}) async-start(bf16[8,2,6144]{2,1,0:T(2,128)(2,1)} %reshape.646), calls=%async_computation.2 | async-start | bytes 393216 | tf_op jit(solution)/shard_map/all_to_all | solution.py:195
  43.4 7.4 %all-to-all-done.2 = bf16[8,2,6144]{2,1,0:T(2,128)(2,1)S(1)} async-done(((bf16[8,2,6144]{2,1,0:T(2,128)(2,1)}), bf16[8,2,6144]{2,1,0:T(2,128)(2,1)S(1)}, u32[]{:S(2)}, u32[]{:S(2)}) %all-to-all-start.2) | async-done | bytes 196640 | tf_op jit(solution)/shard_map/all_to_all | solution.py:195
  50.9 3.3 %all-to-all-start.4 = ((bf16[8,2,768]{2,1,0:T(2,128)(2,1)}), bf16[8,2,768]{2,1,0:T(2,128)(2,1)S(1)}, u32[]{:S(2)}, u32[]{:S(2)}) async-start(bf16[8,2,768]{2,1,0:T(2,128)(2,1)} %reshape.642), calls=%async_computation.4 | async-start | bytes 49152 | tf_op jit(solution)/shard_map/all_to_all | solution.py:197
  56.0 4.7 %collective-permute-start.2 = (bf16[24,8,1536]{2,1,0:T(8,128)(2,1)}, bf16[24,8,1536]{2,1,0:T(8,128)(2,1)}, u32[]{:S(2)}, u32[]{:S(2)}) collective-permute-start(bf16[24,8,1536]{2,1,0:T(8,128)(2,1)} %get-tuple-element.30), channel_id=1, source_target_pairs={{0,1},{1,2},{2,3},{3,4},{4,5},{5,6},{6,7},{8,9},{9,10},{10,11},{11... | collective-permute-start | bytes 1769480 | tf_op jit(solution)/shard_map/ppermute | solution.py:24
  64.6 6.7 %all-to-all-start.6 = ((f32[8,1,256]{2,1,0:T(1,128)}), f32[8,1,256]{2,1,0:T(1,128)S(1)}, u32[]{:S(2)}, u32[]{:S(2)}) async-start(f32[8,1,256]{2,1,0:T(1,128)} %reshape.652), calls=%async_computation.6 | async-start | bytes 16384 | tf_op jit(solution)/shard_map/all_to_all | solution.py:218
  78.4 6.2 %all-to-all-done.6 = f32[8,1,256]{2,1,0:T(1,128)S(1)} async-done(((f32[8,1,256]{2,1,0:T(1,128)}), f32[8,1,256]{2,1,0:T(1,128)S(1)}, u32[]{:S(2)}, u32[]{:S(2)}) %all-to-all-start.6) | async-done | bytes 8224 | tf_op jit(solution)/shard_map/all_to_all | solution.py:218
  84.6 6.5 %all-to-all-start.3 = ((f32[8,1,256]{2,1,0:T(1,128)}), f32[8,1,256]{2,1,0:T(1,128)}, u32[]{:S(2)}, u32[]{:S(2)}) async-start(f32[8,1,256]{2,1,0:T(1,128)} %reshape.650), calls=%async_computation.3 | async-start | bytes 16384 | tf_op jit(solution)/shard_map/all_to_all | solution.py:217
  92.1 1.5 %copy.257 = f32[1,16,128,48]{3,1,0,2:T(8,128)S(1)} copy(f32[1,16,128,48]{2,3,1,0:T(8,128)} %convolution_bitcast_fusion) | data formatting | bytes 786432 | tf_op jit(solution)/shard_map/broadcast_in_dim | solution.py:215
  93.6 1.7 %reshape.648 = f32[8,1,12288]{2,1,0:T(1,128)} reshape(f32[128,1,16,48]{3,2,1,0:T(8,128)S(1)} %bitcast.225) | data formatting | bytes 786432
  97.5 6.0 %all-to-all-start.5 = ((f32[8,1,12288]{2,1,0:T(1,128)}), f32[8,1,12288]{2,1,0:T(1,128)}, u32[]{:S(2)}, u32[]{:S(2)}) async-start(f32[8,1,12288]{2,1,0:T(1,128)} %reshape.648), calls=%async_computation.5 | async-start | bytes 786432 | tf_op jit(solution)/shard_map/all_to_all | solution.py:214
  108.5 1.7 %copy.298 = bf16[768,96]{0,1:T(8,128)(2,1)} copy(bf16[768,96]{1,0:T(8,128)(2,1)} %get-tuple-element.22) | data formatting | bytes 294912
  110.2 1.7 %copy.297 = bf16[768,96]{0,1:T(8,128)(2,1)} copy(bf16[768,96]{1,0:T(8,128)(2,1)} %get-tuple-element.23) | data formatting | bytes 294912
  111.9 1.7 %copy.296 = bf16[768,96]{0,1:T(8,128)(2,1)} copy(bf16[768,96]{1,0:T(8,128)(2,1)} %get-tuple-element.24) | data formatting | bytes 294912
  121.0 1.7 %copy.285 = bf16[768,96]{0,1:T(8,128)(2,1)} copy(bf16[768,96]{1,0:T(8,128)(2,1)} %get-tuple-element.16) | data formatting | bytes 294912
  135.2 2.5 %reduce = f32[8,12288]{1,0:T(8,128)S(1)} reduce(f32[8,1,12288]{2,1,0:T(1,128)} %all-to-all-done.5, f32[]{:T(128)} %broadcast.586), dimensions={1}, to_apply=%all_to_all.102.reduce_sub_computation | reduce | bytes 786436 | tf_op jit(solution)/shard_map/all_to_all | solution.py:214
  (181 shorter events, 54.7 us)
Async XLA Ops:
  0.0 138.9 %copy-start = (bf16[768,768]{1,0:T(8,128)(2,1)S(1)}, bf16[768,768]{1,0:T(8,128)(2,1)}, u32[]{:S(2)}) copy-start(bf16[768,768]{1,0:T(8,128)(2,1)} %param.16) | copy-start | bytes 3538948
  0.0 20.3 %copy-start.31 = (pred[8,16]{1,0:T(8,128)(4,1)S(1)}, pred[8,16]{1,0:T(8,128)(4,1)}, u32[]{:S(2)}) copy-start(pred[8,16]{1,0:T(8,128)(4,1)} %constant.105.clone) | copy-start | bytes 388
  2.0 52.8 %collective-permute-start.1 = (bf16[8,16,1536]{2,1,0:T(8,128)(2,1)S(1)}, bf16[8,16,1536]{2,1,0:T(8,128)(2,1)S(1)}, u32[]{:S(2)}, u32[]{:S(2)}) collective-permute-start(bf16[8,16,1536]{2,1,0:T(8,128)(2,1)S(1)} %constant_dynamic-update-slice_fusion), channel_id=1, source_target_pairs={{8,0},{16,8},{24,16},{9,1},{17,9},{25,17},{10,2},{18,10},{26,18},{... | collective-permute-start | bytes 1179656 | tf_op jit(solution)/shard_map/ppermute | solution.py:25
  3.3 51.5 %collective-permute-start = (bf16[8,16,1536]{2,1,0:T(8,128)(2,1)S(1)}, bf16[8,16,1536]{2,1,0:T(8,128)(2,1)S(1)}, u32[]{:S(2)}, u32[]{:S(2)}) collective-permute-start(bf16[8,16,1536]{2,1,0:T(8,128)(2,1)S(1)} %constant_dynamic-update-slice_fusion), channel_id=1, source_target_pairs={{0,8},{8,16},{16,24},{1,9},{9,17},{17,25},{2,10},{10,18},{18,26},{... | collective-permute-start | bytes 1179656 | tf_op jit(solution)/shard_map/ppermute | solution.py:24
  7.0 19.9 %all-to-all-start = ((s32[8,16,1]{1,2,0:T(1,128)}), s32[8,16,1]{1,2,0:T(1,128)S(1)}, u32[]{:S(2)}, u32[]{:S(2)}) async-start(s32[8,16,1]{1,2,0:T(1,128)} %multiply_add_fusion), calls=%async_computation | async-start | bytes 8192 | tf_op jit(solution)/shard_map/all_to_all | solution.py:198
  20.3 12.6 %copy-start.2 = (s32[16]{0:T(128)S(1)}, s32[16]{0:T(128)}, u32[]{:S(2)}) copy-start(s32[16]{0:T(128)} %param.14) | copy-start | bytes 196
  20.3 13.2 %copy-start.3 = (s32[16]{0:T(128)S(1)}, s32[16]{0:T(128)}, u32[]{:S(2)}) copy-start(s32[16]{0:T(128)} %param.15) | copy-start | bytes 196
  20.3 14.2 %copy-start.1 = (s32[32,128]{1,0:T(8,128)S(1)}, s32[32,128]{1,0:T(8,128)}, u32[]{:S(2)}) copy-start(s32[32,128]{1,0:T(8,128)} %param.13) | copy-start | bytes 49156
  26.8 12.6 %all-to-all-start.1 = ((bf16[8,2,768]{2,1,0:T(2,128)(2,1)}), bf16[8,2,768]{2,1,0:T(2,128)(2,1)S(1)}, u32[]{:S(2)}, u32[]{:S(2)}) async-start(bf16[8,2,768]{2,1,0:T(2,128)(2,1)} %reshape.644), calls=%async_computation.1 | async-start | bytes 49152 | tf_op jit(solution)/shard_map/all_to_all | solution.py:196
  39.4 11.4 %all-to-all-start.2 = ((bf16[8,2,6144]{2,1,0:T(2,128)(2,1)}), bf16[8,2,6144]{2,1,0:T(2,128)(2,1)S(1)}, u32[]{:S(2)}, u32[]{:S(2)}) async-start(bf16[8,2,6144]{2,1,0:T(2,128)(2,1)} %reshape.646), calls=%async_computation.2 | async-start | bytes 393216 | tf_op jit(solution)/shard_map/all_to_all | solution.py:195
  50.9 13.8 %all-to-all-start.4 = ((bf16[8,2,768]{2,1,0:T(2,128)(2,1)}), bf16[8,2,768]{2,1,0:T(2,128)(2,1)S(1)}, u32[]{:S(2)}, u32[]{:S(2)}) async-start(bf16[8,2,768]{2,1,0:T(2,128)(2,1)} %reshape.642), calls=%async_computation.4 | async-start | bytes 49152 | tf_op jit(solution)/shard_map/all_to_all | solution.py:197
  54.9 16.4 %copy-start.5 = (bf16[8,16,768]{2,1,0:T(8,128)(2,1)S(1)}, bf16[8,16,768]{2,1,0:T(8,128)(2,1)}, u32[]{:S(2)}) copy-start(bf16[8,16,768]{2,1,0:T(8,128)(2,1)} %param.10) | copy-start | bytes 589828
  54.9 20.9 %copy-start.4 = (pred[8,16,24,32]{3,2,1,0:T(8,128)(4,1)S(1)}, pred[8,16,24,32]{3,2,1,0:T(8,128)(4,1)}, u32[]{:S(2)}) copy-start(pred[8,16,24,32]{3,2,1,0:T(8,128)(4,1)} %and_or_fusion) | copy-start | bytes 294916
  56.0 49.7 %collective-permute-start.2 = (bf16[24,8,1536]{2,1,0:T(8,128)(2,1)}, bf16[24,8,1536]{2,1,0:T(8,128)(2,1)}, u32[]{:S(2)}, u32[]{:S(2)}) collective-permute-start(bf16[24,8,1536]{2,1,0:T(8,128)(2,1)} %get-tuple-element.30), channel_id=1, source_target_pairs={{0,1},{1,2},{2,3},{3,4},{4,5},{5,6},{6,7},{8,9},{9,10},{10,11},{11... | collective-permute-start | bytes 1769480 | tf_op jit(solution)/shard_map/ppermute | solution.py:24
  60.7 45.0 %collective-permute-start.3 = (bf16[24,8,1536]{2,1,0:T(8,128)(2,1)}, bf16[24,8,1536]{2,1,0:T(8,128)(2,1)}, u32[]{:S(2)}, u32[]{:S(2)}) collective-permute-start(bf16[24,8,1536]{2,1,0:T(8,128)(2,1)} %get-tuple-element.31), channel_id=1, source_target_pairs={{1,0},{2,1},{3,2},{4,3},{5,4},{6,5},{7,6},{9,8},{10,9},{11,10},{12... | collective-permute-start | bytes 1769480 | tf_op jit(solution)/shard_map/ppermute | solution.py:25
  64.6 19.9 %all-to-all-start.6 = ((f32[8,1,256]{2,1,0:T(1,128)}), f32[8,1,256]{2,1,0:T(1,128)S(1)}, u32[]{:S(2)}, u32[]{:S(2)}) async-start(f32[8,1,256]{2,1,0:T(1,128)} %reshape.652), calls=%async_computation.6 | async-start | bytes 16384 | tf_op jit(solution)/shard_map/all_to_all | solution.py:218
  84.6 6.5 %copy-start.24 = (f32[8,1,256]{2,1,0:T(1,128)}, f32[8,1,256]{2,1,0:T(1,128)S(1)}, u32[]{:S(2)}) copy-start(f32[8,1,256]{2,1,0:T(1,128)S(1)} %all-to-all-done.6) | copy-start | bytes 24580
  84.6 13.0 %all-to-all-start.3 = ((f32[8,1,256]{2,1,0:T(1,128)}), f32[8,1,256]{2,1,0:T(1,128)}, u32[]{:S(2)}, u32[]{:S(2)}) async-start(f32[8,1,256]{2,1,0:T(1,128)} %reshape.650), calls=%async_computation.3 | async-start | bytes 16384 | tf_op jit(solution)/shard_map/all_to_all | solution.py:217
  97.5 37.6 %all-to-all-start.5 = ((f32[8,1,12288]{2,1,0:T(1,128)}), f32[8,1,12288]{2,1,0:T(1,128)}, u32[]{:S(2)}, u32[]{:S(2)}) async-start(f32[8,1,12288]{2,1,0:T(1,128)} %reshape.648), calls=%async_computation.5 | async-start | bytes 786432 | tf_op jit(solution)/shard_map/all_to_all | solution.py:214
  117.6 6.4 %copy-start.21 = (bf16[128,96]{0,1:T(8,128)(2,1)S(1)}, bf16[128,96]{0,1:T(8,128)(2,1)}, u32[]{:S(2)}) copy-start(bf16[128,96]{0,1:T(8,128)(2,1)} %copy.276) | copy-start | bytes 73732
  118.9 5.6 %copy-start.20 = (bf16[128,96]{0,1:T(8,128)(2,1)S(1)}, bf16[128,96]{0,1:T(8,128)(2,1)}, u32[]{:S(2)}) copy-start(bf16[128,96]{0,1:T(8,128)(2,1)} %copy.278) | copy-start | bytes 73732
  124.0 2.7 %copy-start.14 = (bf16[768,96]{0,1:T(8,128)(2,1)S(1)}, bf16[768,96]{0,1:T(8,128)(2,1)}, u32[]{:S(2)}) copy-start(bf16[768,96]{0,1:T(8,128)(2,1)} %copy.292) | copy-start | bytes 442372
  124.4 2.6 %copy-start.19 = (bf16[128,96]{0,1:T(8,128)(2,1)S(1)}, bf16[128,96]{0,1:T(8,128)(2,1)}, u32[]{:S(2)}) copy-start(bf16[128,96]{0,1:T(8,128)(2,1)} %copy.280) | copy-start | bytes 73732
  124.8 2.6 %copy-start.18 = (bf16[128,96]{0,1:T(8,128)(2,1)S(1)}, bf16[128,96]{0,1:T(8,128)(2,1)}, u32[]{:S(2)}) copy-start(bf16[128,96]{0,1:T(8,128)(2,1)} %copy.282) | copy-start | bytes 73732
  (19 other events, 32.7 us)
where the time goes:
time: 141 us; the launch traced here: 140 us
  starting transfers between devices  49.4 us (35%)
  local copies, waits for them, and re-layouts  46.4 us (33%)
  other arithmetic  17.5 us (12%)
  waiting for transfers between devices  16.4 us (12%)
  matrix products  9.44 us (7%)
    unnamed x101, local copies, waits for them, and re-layouts  27.4 us
    ppermute x2, starting transfers between devices, padded_2(): before = lax.ppermute(last, axis, up)  7.71 us
    all_to_all x1, waiting for transfers between devices, per_device(): lax.all_to_all(q_send, 'col', split_axis=0, concat_axis=2, tiled=True)  7.45 us
    all_to_all x1, starting transfers between devices, per_device(): lax.all_to_all(id_send, 'col', split_axis=0, concat_axis=2, tiled=True)  7.25 us
    all_to_all x1, starting transfers between devices, per_device(): lax.all_to_all(totals[None], 'col', split_axis=2, concat_axis=0, tiled=True)  6.69 us
    all_to_all x1, starting transfers between devices, per_device(): lax.all_to_all(highest[None], 'col', split_axis=2, concat_axis=0, tiled=T...  6.46 us
    all_to_all x1, waiting for transfers between devices, per_device(): lax.all_to_all(totals[None], 'col', split_axis=2, concat_axis=0, tiled=True)  6.17 us
    all_to_all x1, starting transfers between devices, per_device(): lax.all_to_all(k_send, 'col', split_axis=0, concat_axis=2, tiled=True)  6 us
  transfers between devices with their start and end apart: 11, of which 3 were waited for; matrix products, arithmetic and copies ran while one was open for 48% of the time, Pallas kernels for 0%

commit v1 on v0

v1 whole, which is shorter than its diff:
```python
import functools
import math

import jax
import jax.numpy as jnp
from jax import lax
from jax.experimental import pallas as pl
from jax.experimental.pallas import tpu as pltpu
from jax.sharding import PartitionSpec as P

HEAD_COUNT = 16
R = 8
DILATION_MIN = 8
NEG_FILL = -1e30
MESH = pl.DeviceIdType.MESH
HEADS_TOGETHER = 4
F32 = jnp.float32
BF16 = jnp.bfloat16


def iota(shape, dim):
    return lax.broadcasted_iota(jnp.int32, shape, dim)


def one_hot(condition):
    return jnp.where(condition, 1.0, 0.0).astype(BF16)


def lane_window(group, head_dimension):
    first = group * HEADS_TOGETHER * head_dimension
    return first // 128 * 128, first % 128


def head_mask(group, head, head_dimension):
    _, offset = lane_window(group, head_dimension)
    lane = iota((1, 256), 1) - offset - head * head_dimension
    return (lane >= 0) & (lane < head_dimension)


def gathered_tissue(tissue, key_rows, key_cols):
    rows, cols = tissue.shape
    n = key_rows.shape[1]
    pick = one_hot(iota((cols, n), 0) == key_cols)
    by_col = jnp.dot(tissue, pick, preferred_element_type=F32)
    keep = iota((rows, n), 0) == key_rows
    return jnp.sum(jnp.where(keep, by_col, 0.0), axis=0, keepdims=True)


def window_bias(tissue, key_rel_row, key_rel_col, row_offset, column_offset, dr, dc):
    present = gathered_tissue(tissue, key_rel_row + row_offset, key_rel_col + column_offset)
    n = key_rel_row.shape[1]
    q = iota((dr * dc, n), 0)
    row_gap = jnp.abs(key_rel_row - q // dc)
    col_gap = jnp.abs(key_rel_col - q % dc)
    near = (row_gap <= R) & (col_gap <= R) & (present > 0.5)
    self_key = (row_gap + col_gap) == 0
    return jnp.where(near | self_key, 0.0, NEG_FILL)


def kernel(
    n_row, n_col, dr, dc,
    q_hbm, k_hbm, v_hbm, tissue_ref, dil_ref, seg_ref, w_hbm, out_ref,
    q_ref, w_ref, near_kv, far_kv, halves, chosen, bias_a, bias_b, tissue_dil,
    num_a, max_a, sum_a, local_sem, send_sem, recv_sem, dil_send, dil_recv,
):
    row, col = lax.axis_index("row"), lax.axis_index("col")
    tiles, width = q_ref.shape
    hd = width // HEAD_COUNT
    half = tiles // 2
    win_far = 6 * half
    sel = tiles // DILATION_MIN

    loads = [
        pltpu.make_async_copy(k_hbm, near_kv.at[0, pl.ds(0, tiles)], local_sem.at[0]),
        pltpu.make_async_copy(v_hbm, near_kv.at[1, pl.ds(0, tiles)], local_sem.at[1]),
        pltpu.make_async_copy(q_hbm, q_ref, local_sem.at[2]),
        pltpu.make_async_copy(w_hbm, w_ref, local_sem.at[3]),
    ]
    for load in loads:
        load.start()

    has_up, has_down = row > 0, row < n_row - 1
    has_left, has_right = col > 0, col < n_col - 1
    up = (lax.rem(row + n_row - 1, n_row), col)
    down = (lax.rem(row + 1, n_row), col)
    left = (row, lax.rem(col + n_col - 1, n_col))
    right = (row, lax.rem(col + 1, n_col))

    barrier = pltpu.get_barrier_semaphore()

    @pl.when(has_up)
    def _():
        pl.semaphore_signal(barrier, inc=1, device_id=up, device_id_type=MESH)

    @pl.when(has_down)
    def _():
        pl.semaphore_signal(barrier, inc=1, device_id=down, device_id_type=MESH)

    for d in range(1, n_col):
        peer = (row, lax.rem(col + d, n_col))
        pl.semaphore_signal(barrier, inc=1, device_id=peer, device_id_type=MESH)

    def remote(src, dst, kind, device):
        return pltpu.make_async_remote_copy(
            src_ref=src, dst_ref=dst, send_sem=send_sem.at[kind], recv_sem=recv_sem.at[kind],
            device_id=device, device_id_type=MESH,
        )

    def near_rows(first, count):
        return near_kv.at[:, pl.ds(first, count)]

    def far_rows(first, count):
        return far_kv.at[:, pl.ds(first, count)]

    own = near_rows(0, tiles)
    to_up = remote(own, near_rows(2 * tiles, tiles), 0, up)
    to_down = remote(own, near_rows(tiles, tiles), 1, down)
    to_left = remote(halves.at[:, pl.ds(0, half)], far_rows(half, half), 2, left)
    to_right = remote(halves.at[:, pl.ds(half, half)], far_rows(0, half), 3, right)
    left_to_up = remote(far_rows(0, half), far_rows(4 * half, half), 4, up)
    left_to_down = remote(far_rows(0, half), far_rows(2 * half, half), 5, down)
    right_to_up = remote(far_rows(half, half), far_rows(5 * half, half), 6, up)
    right_to_down = remote(far_rows(half, half), far_rows(3 * half, half), 7, down)

    i, j = iota((tiles, tiles), 0), iota((tiles, tiles), 1)
    within = i % half
    split_order = one_hot(j == within // R * dc + (i // half) * R + within % R)
    local_sel = dc // DILATION_MIN
    s = i % sel
    phase_order = one_hot(j == s // local_sel * dc + s % local_sel * DILATION_MIN + i // sel)
    lane_phase = iota((1, width), 1) // hd % DILATION_MIN
    slot = pl.ds(pl.multiple_of(win_far + col * sel, sel), sel)

    loads[0].wait()
    loads[1].wait()
    for t in range(2):
        mine = near_kv[t, pl.ds(0, tiles)]
        halves[t] = jnp.dot(split_order, mine, preferred_element_type=F32).astype(BF16)
    pl.semaphore_wait(
        barrier,
        (n_col - 1) + jnp.where(has_up, 1, 0) + jnp.where(has_down, 1, 0),
    )
    pl.when(has_left)(to_left.start)
    pl.when(has_right)(to_right.start)
    pl.when(has_up)(to_up.start)
    pl.when(has_down)(to_down.start)
    for t in range(2):
        mine = near_kv[t, pl.ds(0, tiles)]
        by_phase = jnp.dot(phase_order, mine, preferred_element_type=F32)
        picked = jnp.zeros((sel, width), F32)
        for p in range(DILATION_MIN):
            picked += jnp.where(lane_phase == p, by_phase[p * sel:(p + 1) * sel], 0.0)
        picked = picked.astype(BF16)
        chosen[t] = picked
        far_kv[t, slot] = picked
    dil = []
    for d in range(1, n_col):
        copy = pltpu.make_async_remote_copy(
            src_ref=chosen, dst_ref=far_kv.at[:, slot],
            send_sem=dil_send.at[d], recv_sem=dil_recv.at[d],
            device_id=(row, lax.rem(col + d, n_col)), device_id_type=MESH,
        )
        copy.start()
        dil.append(copy)

    def clear_near(first):
        near_kv[:, pl.ds(first, tiles)] = jnp.zeros((2, tiles, width), BF16)

    def clear_far(first):
        far_kv[:, pl.ds(first, half)] = jnp.zeros((2, half, width), BF16)

    @pl.when(jnp.logical_not(has_up))
    def _():
        clear_near(tiles)

    @pl.when(jnp.logical_not(has_down))
    def _():
        clear_near(2 * tiles)

    for side, has_side in ((0, has_left), (1, has_right)):
        for block, has_block in ((0, None), (1, has_up), (2, has_down)):
            have = has_side if has_block is None else has_side & has_block

            @pl.when(jnp.logical_not(have))
            def _(side=side, block=block):
                clear_far((2 * block + side) * half)

    tissue = tissue_ref[...].astype(F32).astype(BF16)
    row_offset, column_offset = row * dr, col * dc
    k = iota((1, 3 * tiles), 1)
    block = k // tiles
    shift = jnp.where(block == 1, -dr, jnp.where(block == 2, dr, 0))
    inner = k % tiles
    bias_a[...] = window_bias(
        tissue, inner // dc + shift, inner % dc, row_offset, column_offset, dr, dc
    )
    within = inner % half
    far_col = jnp.where(inner >= half, dc, -R) + within % R
    bias_b[...] = window_bias(
        tissue, within // R + shift, far_col, row_offset, column_offset, dr, dc
    )
    n_dil = sel * n_col
    kd = iota((1, n_dil), 1)
    dil_row = kd % sel // local_sel
    dil_col = kd // sel * dc + kd % local_sel * DILATION_MIN
    for p in range(DILATION_MIN):
        tissue_dil[pl.ds(p, 1)] = gathered_tissue(tissue, dil_row + row_offset, dil_col + p)

    @pl.when(has_left)
    def _():
        to_right.wait_recv()
        pl.when(has_up)(left_to_up.start)
        pl.when(has_down)(left_to_down.start)

    @pl.when(has_right)
    def _():
        to_left.wait_recv()
        pl.when(has_up)(right_to_up.start)
        pl.when(has_down)(right_to_down.start)

    pl.when(has_down)(to_up.wait_recv)
    pl.when(has_up)(to_down.wait_recv)
    loads[2].wait()

    factor = math.log2(math.e) / math.sqrt(hd)
    groups = HEAD_COUNT // HEADS_TOGETHER
    stacked = HEADS_TOGETHER * tiles

    def stacked_queries(g):
        base, _ = lane_window(g, hd)
        query = q_ref[:, pl.ds(base, 256)]
        return jnp.concatenate(
            [
                jnp.where(head_mask(g, h, hd), query, jnp.zeros_like(query))
                for h in range(HEADS_TOGETHER)
            ],
            axis=0,
        )

    def scores(g, kv, first, count):
        base, _ = lane_window(g, hd)
        keys = kv[0, pl.ds(first, count), pl.ds(base, 256)]
        raw = lax.dot_general(
            stacked_queries(g), keys, (((1,), (1,)), ((), ())), preferred_element_type=F32
        )
        return raw.reshape(HEADS_TOGETHER, tiles, count)

    for g in range(groups):
        base, _ = lane_window(g, hd)
        s = scores(g, near_kv, 0, 3 * tiles) + bias_a[...][None]
        top = jnp.max(s, axis=-1, keepdims=True)
        p = jnp.exp2((s - top) * factor)
        max_a[g] = top.reshape(stacked, 1)
        sum_a[g] = jnp.sum(p, axis=-1, keepdims=True).reshape(stacked, 1)
        num_a[g] = jnp.dot(
            p.astype(BF16).reshape(stacked, 3 * tiles),
            near_kv[1, :, pl.ds(base, 256)],
            preferred_element_type=F32,
        )

    q_idx = iota((tiles, n_dil), 0)
    q_col = column_offset + q_idx % dc
    same_row = dil_row == q_idx // dc
    for copy in dil:
        copy.wait_recv()

    @pl.when(has_left)
    def _():
        pl.when(has_up)(left_to_down.wait_recv)
        pl.when(has_down)(left_to_up.wait_recv)

    @pl.when(has_right)
    def _():
        pl.when(has_up)(right_to_down.wait_recv)
        pl.when(has_down)(right_to_up.wait_recv)

    parts = []
    for g in range(groups):
        base, _ = lane_window(g, hd)
        s_win = scores(g, far_kv, 0, win_far) + bias_b[...][None]
        s_dil = scores(g, far_kv, win_far, n_dil)
        masked = []
        for h in range(HEADS_TOGETHER):
            head = g * HEADS_TOGETHER + h
            stride = jnp.left_shift(jnp.int32(DILATION_MIN), dil_ref[head])
            segment = jnp.right_shift(jnp.int32(dc * n_col), seg_ref[head])
            key_col = dil_col + head % DILATION_MIN
            present = tissue_dil[pl.ds(head % DILATION_MIN, 1)] > 0.5
            key_ok = present & ((key_col & (stride - 1)) == (head & (stride - 1)))
            ok = key_ok & same_row & ((key_col ^ q_col) < segment)
            masked.append(jnp.where(ok, s_dil[h], NEG_FILL)[None])
        s_dil = jnp.concatenate(masked, axis=0)
        old_top = max_a[g].reshape(HEADS_TOGETHER, tiles, 1)
        top = jnp.maximum(
            jnp.maximum(
                jnp.max(s_win, axis=-1, keepdims=True), jnp.max(s_dil, axis=-1, keepdims=True)
            ),
            old_top,
        )
        p_win = jnp.exp2((s_win - top) * factor)
        p_dil = jnp.exp2((s_dil - top) * factor)
        keep = jnp.exp2((old_top - top) * factor).reshape(stacked, 1)
        total = (
            keep * sum_a[g]
            + jnp.sum(p_win, axis=-1, keepdims=True).reshape(stacked, 1)
            + jnp.sum(p_dil, axis=-1, keepdims=True).reshape(stacked, 1)
        )
        numer = (
            keep * num_a[g]
            + jnp.dot(
                p_win.astype(BF16).reshape(stacked, win_far),
                far_kv[1, pl.ds(0, win_far), pl.ds(base, 256)],
                preferred_element_type=F32,
            )
            + jnp.dot(
                p_dil.astype(BF16).reshape(stacked, n_dil),
                far_kv[1, pl.ds(win_far, n_dil), pl.ds(base, 256)],
                preferred_element_type=F32,
            )
        )
        mixed = numer / total
        together = jnp.zeros((tiles, 256), F32)
        for h in range(HEADS_TOGETHER):
            together += jnp.where(
                head_mask(g, h, hd), mixed[h * tiles:(h + 1) * tiles], 0.0
            )
        parts.append(together)

    lanes = []
    for g in range(0, groups, 2):
        a, b = parts[g], parts[g + 1]
        lanes += [a[:, :128], a[:, 128:] + b[:, :128], b[:, 128:]]
    attended = jnp.concatenate(lanes, axis=1).astype(BF16)
    loads[3].wait()
    out_ref[...] = jnp.dot(attended, w_ref[...], preferred_element_type=F32).astype(BF16)

    pl.when(has_left)(to_left.wait_send)
    pl.when(has_right)(to_right.wait_send)
    pl.when(has_up)(to_up.wait_send)
    pl.when(has_down)(to_down.wait_send)
    pl.when(has_left & has_up)(left_to_up.wait_send)
    pl.when(has_left & has_down)(left_to_down.wait_send)
    pl.when(has_right & has_up)(right_to_up.wait_send)
    pl.when(has_right & has_down)(right_to_down.wait_send)
    for copy in dil:
        copy.wait_send()


def solution(mesh):
    n_row, n_col = mesh.shape["row"], mesh.shape["col"]

    def per_device(q, k, v, tissue, dilation_levels, segment_levels, output_matrix):
        dr, dc, width = q.shape
        tiles = dr * dc
        sel = tiles // DILATION_MIN
        groups = HEAD_COUNT // HEADS_TOGETHER
        stacked = HEADS_TOGETHER * tiles
        any_space = pl.BlockSpec(memory_space=pl.ANY)
        vmem = pl.BlockSpec(memory_space=pltpu.VMEM)
        smem = pl.BlockSpec(memory_space=pltpu.SMEM)
        out = pl.pallas_call(
            functools.partial(kernel, n_row, n_col, dr, dc),
            out_shape=jax.ShapeDtypeStruct((tiles, width), BF16),
            in_specs=[any_space, any_space, any_space, vmem, smem, smem, any_space],
            out_specs=vmem,
            scratch_shapes=[
                pltpu.VMEM((tiles, width), BF16),
                pltpu.VMEM(output_matrix.shape, BF16),
                pltpu.VMEM((2, 3 * tiles, width), BF16),
                pltpu.VMEM((2, 3 * tiles + sel * n_col, width), BF16),
                pltpu.VMEM((2, tiles, width), BF16),
                pltpu.VMEM((2, sel, width), BF16),
                pltpu.VMEM((tiles, 3 * tiles), F32),
                pltpu.VMEM((tiles, 3 * tiles), F32),
                pltpu.VMEM((DILATION_MIN, sel * n_col), F32),
                pltpu.VMEM((groups, stacked, 256), F32),
                pltpu.VMEM((groups, stacked, 1), F32),
                pltpu.VMEM((groups, stacked, 1), F32),
                pltpu.SemaphoreType.DMA((4,)),
                pltpu.SemaphoreType.DMA((8,)),
                pltpu.SemaphoreType.DMA((8,)),
                pltpu.SemaphoreType.DMA((n_col,)),
                pltpu.SemaphoreType.DMA((n_col,)),
            ],
            compiler_params=pltpu.CompilerParams(
                collective_id=0, has_side_effects=True, vmem_limit_bytes=56 * 1024 * 1024
            ),
        )(
            q.reshape(tiles, width), k.reshape(tiles, width), v.reshape(tiles, width),
            tissue, dilation_levels, segment_levels, output_matrix,
        )
        return out.reshape(dr, dc, width)

    split = P("row", "col", None)
    return jax.shard_map(
        per_device,
        mesh=mesh,
        in_specs=(split, split, split, P(), P(), P(), P()),
        out_specs=split,
        check_vma=False,
    )
```

time: 141 us -> 32.7 us (0.23)
  the two profiles are of different devices: /device:TPU:0 before, /device:TPU:3 now
where the time goes in v1:
time: 32.7 us; the launch traced here: 32.5 us
  Pallas kernels  30.8 us (94%)
  local copies, waits for them, and re-layouts  1.62 us (5%)
    pallas_call x1, Pallas kernels, per_device(): pl.pallas_call(functools.partial(kernel, n_row, n_col, dr, dc), out_shape...  30.8 us
    unnamed x1, local copies, waits for them, and re-layouts  1.62 us

profile of v1, /device:TPU:3, one launch (start us, length us, event | category | flops | bytes accessed | tf_op | source)
XLA Modules:
  0.0 32.5 jit_solution(14726407764068462632)
XLA Ops:
  0.0 30.8 %shard_map.73 = bf16[128,768]{1,0:T(8,128)(2,1)} custom-call(bf16[128,768]{1,0:T(8,128)(2,1)} %bitcast.5, bf16[128,768]{1,0:T(8,128)(2,1)} %bitcast.6, bf16[128,768]{1,0:T(8,128)(2,1)} %bitcast.7, s32[32,128]{1,0:T(8,128)} %tissue_ref.1, s32[16]{0:T(128)} %dil_ref.1, s32[16]{0:T(128)} %seg_ref.1, bf16[768,768]{1,0:T(8,128)(2,1)} %w_hbm.1), custom_call_target="tpu_custom_call" | custom-call | tf_op jit(solution)/shard_map/pallas_call | solution.py:361
  30.8 1.6 %copy.9 = bf16[8,16,768]{2,1,0:T(8,128)(2,1)} copy(bf16[8,16,768]{2,1,0:T(8,128)(2,1)} %bitcast.4) | data formatting | bytes 393216

commit v2 on v1

v2 whole, which is shorter than its diff:
```python
import functools
import math

import jax
import jax.numpy as jnp
from jax import lax
from jax.experimental import pallas as pl
from jax.experimental.pallas import tpu as pltpu
from jax.sharding import PartitionSpec as P

HEAD_COUNT = 16
R = 8
DILATION_MIN = 8
NEG_FILL = -1e30
MESH = pl.DeviceIdType.MESH
HEADS_TOGETHER = 4
F32 = jnp.float32
BF16 = jnp.bfloat16


def iota(shape, dim):
    return lax.broadcasted_iota(jnp.int32, shape, dim)


def one_hot(condition):
    return jnp.where(condition, 1.0, 0.0).astype(BF16)


def lane_window(group, head_dimension):
    first = group * HEADS_TOGETHER * head_dimension
    return first // 128 * 128, first % 128


def head_mask(group, head, head_dimension):
    _, offset = lane_window(group, head_dimension)
    lane = iota((1, 256), 1) - offset - head * head_dimension
    return (lane >= 0) & (lane < head_dimension)


def gathered_tissue(tissue, key_rows, key_cols):
    rows, cols = tissue.shape
    n = key_rows.shape[1]
    pick = one_hot(iota((cols, n), 0) == key_cols)
    by_col = jnp.dot(tissue, pick, preferred_element_type=F32)
    keep = iota((rows, n), 0) == key_rows
    return jnp.sum(jnp.where(keep, by_col, 0.0), axis=0, keepdims=True)


def window_bias(tissue, key_rel_row, key_rel_col, row_offset, column_offset, dr, dc):
    present = gathered_tissue(tissue, key_rel_row + row_offset, key_rel_col + column_offset)
    n = key_rel_row.shape[1]
    q = iota((dr * dc, n), 0)
    row_gap = jnp.abs(key_rel_row - q // dc)
    col_gap = jnp.abs(key_rel_col - q % dc)
    near = (row_gap <= R) & (col_gap <= R) & (present > 0.5)
    self_key = (row_gap + col_gap) == 0
    return jnp.where(near | self_key, 0.0, NEG_FILL)


def kernel(
    n_row, n_col, dr, dc,
    q_hbm, k_hbm, v_hbm, tissue_ref, dil_ref, seg_ref, out_ref,
    q_ref, own_kv, mid_kv, far_kv, halves, chosen, bias_own, bias_mid, bias_far,
    numer, highest, total, local_sem, send_sem, recv_sem, dil_send, dil_recv,
):
    row, col = lax.axis_index("row"), lax.axis_index("col")
    tiles, width = q_ref.shape
    hd = width // HEAD_COUNT
    half = tiles // 2
    corners = 4 * half
    sel = tiles // DILATION_MIN

    loads = [
        pltpu.make_async_copy(k_hbm, own_kv.at[0], local_sem.at[0]),
        pltpu.make_async_copy(v_hbm, own_kv.at[1], local_sem.at[1]),
        pltpu.make_async_copy(q_hbm, q_ref, local_sem.at[2]),
    ]
    for load in loads:
        load.start()

    has_up, has_down = row > 0, row < n_row - 1
    has_left, has_right = col > 0, col < n_col - 1
    up = (lax.rem(row + n_row - 1, n_row), col)
    down = (lax.rem(row + 1, n_row), col)
    left = (row, lax.rem(col + n_col - 1, n_col))
    right = (row, lax.rem(col + 1, n_col))

    barrier = pltpu.get_barrier_semaphore()

    @pl.when(has_up)
    def _():
        pl.semaphore_signal(barrier, inc=1, device_id=up, device_id_type=MESH)

    @pl.when(has_down)
    def _():
        pl.semaphore_signal(barrier, inc=1, device_id=down, device_id_type=MESH)

    for d in range(1, n_col):
        peer = (row, lax.rem(col + d, n_col))
        pl.semaphore_signal(barrier, inc=1, device_id=peer, device_id_type=MESH)

    def remote(src, dst, kind, device):
        return pltpu.make_async_remote_copy(
            src_ref=src, dst_ref=dst, send_sem=send_sem.at[kind], recv_sem=recv_sem.at[kind],
            device_id=device, device_id_type=MESH,
        )

    def mid(first, count):
        return mid_kv.at[:, pl.ds(first, count)]

    def corner(index):
        return far_kv.at[:, pl.ds(index * half, half)]

    left_here, right_here = mid(2 * tiles, half), mid(2 * tiles + half, half)
    to_up = remote(own_kv, mid(tiles, tiles), 0, up)
    to_down = remote(own_kv, mid(0, tiles), 1, down)
    to_left = remote(halves.at[:, pl.ds(0, half)], right_here, 2, left)
    to_right = remote(halves.at[:, pl.ds(half, half)], left_here, 3, right)
    left_to_up = remote(left_here, corner(2), 4, up)
    left_to_down = remote(left_here, corner(0), 5, down)
    right_to_up = remote(right_here, corner(3), 6, up)
    right_to_down = remote(right_here, corner(1), 7, down)

    i, j = iota((tiles, tiles), 0), iota((tiles, tiles), 1)
    within = i % half
    split_order = one_hot(j == within // R * dc + (i // half) * R + within % R)
    local_sel = dc // DILATION_MIN
    s = i % sel
    phase_order = one_hot(j == s // local_sel * dc + s % local_sel * DILATION_MIN + i // sel)
    lane_phase = iota((1, width), 1) // hd % DILATION_MIN
    slot = pl.ds(pl.multiple_of(corners + col * sel, sel), sel)

    loads[0].wait()
    loads[1].wait()
    for t in range(2):
        halves[t] = jnp.dot(split_order, own_kv[t], preferred_element_type=F32).astype(BF16)
    pl.semaphore_wait(
        barrier,
        (n_col - 1) + jnp.where(has_up, 1, 0) + jnp.where(has_down, 1, 0),
    )
    pl.when(has_left)(to_left.start)
    pl.when(has_right)(to_right.start)
    pl.when(has_up)(to_up.start)
    pl.when(has_down)(to_down.start)
    for t in range(2):
        by_phase = jnp.dot(phase_order, own_kv[t], preferred_element_type=F32)
        picked = jnp.zeros((sel, width), F32)
        for p in range(DILATION_MIN):
            picked += jnp.where(lane_phase == p, by_phase[p * sel:(p + 1) * sel], 0.0)
        picked = picked.astype(BF16)
        chosen[t] = picked
        far_kv[t, slot] = picked
    dil = []
    for d in range(1, n_col):
        copy = pltpu.make_async_remote_copy(
            src_ref=chosen, dst_ref=far_kv.at[:, slot],
            send_sem=dil_send.at[d], recv_sem=dil_recv.at[d],
            device_id=(row, lax.rem(col + d, n_col)), device_id_type=MESH,
        )
        copy.start()
        dil.append(copy)

    def clear(ref, first, count):
        ref[:, pl.ds(first, count)] = jnp.zeros((2, count, width), BF16)

    for ref, first, count, have in (
        (mid_kv, 0, tiles, has_up),
        (mid_kv, tiles, tiles, has_down),
        (mid_kv, 2 * tiles, half, has_left),
        (mid_kv, 2 * tiles + half, half, has_right),
        (far_kv, 0, half, has_up & has_left),
        (far_kv, half, half, has_up & has_right),
        (far_kv, 2 * half, half, has_down & has_left),
        (far_kv, 3 * half, half, has_down & has_right),
    ):
        pl.when(jnp.logical_not(have))(functools.partial(clear, ref, first, count))

    tissue = tissue_ref[...].astype(F32).astype(BF16)
    row_offset, column_offset = row * dr, col * dc

    def bias(key_row, key_col):
        return window_bias(tissue, key_row, key_col, row_offset, column_offset, dr, dc)

    def half_col(k):
        return jnp.where(k % tiles >= half, dc, -R) + k % R

    k = iota((1, tiles), 1)
    bias_own[...] = bias(k // dc, k % dc)
    for block, shift in ((0, -dr), (1, dr)):
        bias_mid[:, pl.ds(block * tiles, tiles)] = bias(k // dc + shift, k % dc)
    bias_mid[:, pl.ds(2 * tiles, tiles)] = bias(k % half // R, half_col(k))

    factor = math.log2(math.e) / math.sqrt(hd)
    groups = HEAD_COUNT // HEADS_TOGETHER
    stacked = HEADS_TOGETHER * tiles

    def attend(g, kv, extra, before):
        base, _ = lane_window(g, hd)
        query = q_ref[:, pl.ds(base, 256)]
        query = jnp.concatenate(
            [
                jnp.where(head_mask(g, h, hd), query, jnp.zeros_like(query))
                for h in range(HEADS_TOGETHER)
            ],
            axis=0,
        )
        scores = lax.dot_general(
            query, kv[0, :, pl.ds(base, 256)], (((1,), (1,)), ((), ())),
            preferred_element_type=F32,
        )
        scores = scores.reshape(HEADS_TOGETHER, tiles, kv.shape[1]) + extra
        scores = scores.reshape(stacked, kv.shape[1])
        top = jnp.max(scores, axis=-1, keepdims=True)
        if before is not None:
            old_numer, old_top, old_total = before
            top = jnp.maximum(top, old_top)
        probs = jnp.exp2((scores - top) * factor)
        new_total = jnp.sum(probs, axis=-1, keepdims=True)
        new_numer = jnp.dot(
            probs.astype(BF16), kv[1, :, pl.ds(base, 256)], preferred_element_type=F32
        )
        if before is not None:
            keep = jnp.exp2((old_top - top) * factor)
            new_total += keep * old_total
            new_numer += keep * old_numer
        return new_numer, top, new_total

    loads[2].wait()
    for g in range(groups):
        numer[g], highest[g], total[g] = attend(g, own_kv, bias_own[...][None], None)

    @pl.when(has_left)
    def _():
        to_right.wait_recv()
        pl.when(has_up)(left_to_up.start)
        pl.when(has_down)(left_to_down.start)

    @pl.when(has_right)
    def _():
        to_left.wait_recv()
        pl.when(has_up)(right_to_up.start)
        pl.when(has_down)(right_to_down.start)

    for block, shift in ((0, -dr), (1, dr)):
        bias_far[0, :, pl.ds(block * tiles, tiles)] = bias(k % half // R + shift, half_col(k))
    for h in range(1, HEAD_COUNT):
        bias_far[h, :, pl.ds(0, corners)] = bias_far[0, :, pl.ds(0, corners)]
    n_dil = sel * n_col
    kd = iota((1, n_dil), 1)
    dil_row = kd % sel // local_sel
    dil_col = kd // sel * dc + kd % local_sel * DILATION_MIN
    q_idx = iota((tiles, n_dil), 0)
    q_col = column_offset + q_idx % dc
    same_row = dil_row == q_idx // dc
    for p in range(DILATION_MIN):
        key_col = dil_col + p
        present = gathered_tissue(tissue, dil_row + row_offset, key_col) > 0.5
        apart = key_col ^ q_col
        for head in range(p, HEAD_COUNT, DILATION_MIN):
            stride = jnp.left_shift(jnp.int32(DILATION_MIN), dil_ref[head])
            segment = jnp.right_shift(jnp.int32(dc * n_col), seg_ref[head])
            key_ok = present & ((key_col & (stride - 1)) == (head & (stride - 1)))
            ok = key_ok & same_row & (apart < segment)
            bias_far[head, :, pl.ds(corners, n_dil)] = jnp.where(ok, 0.0, NEG_FILL)

    pl.when(has_down)(to_up.wait_recv)
    pl.when(has_up)(to_down.wait_recv)
    for g in range(groups):
        numer[g], highest[g], total[g] = attend(
            g, mid_kv, bias_mid[...][None], (numer[g], highest[g], total[g])
        )

    for copy in dil:
        copy.wait_recv()

    @pl.when(has_left)
    def _():
        pl.when(has_up)(left_to_down.wait_recv)
        pl.when(has_down)(left_to_up.wait_recv)

    @pl.when(has_right)
    def _():
        pl.when(has_up)(right_to_down.wait_recv)
        pl.when(has_down)(right_to_up.wait_recv)

    parts = []
    for g in range(groups):
        heads = pl.ds(g * HEADS_TOGETHER, HEADS_TOGETHER)
        top_numer, _, top_total = attend(
            g, far_kv, bias_far[heads], (numer[g], highest[g], total[g])
        )
        mixed = top_numer * (1.0 / top_total)
        together = jnp.zeros((tiles, 256), F32)
        for h in range(HEADS_TOGETHER):
            together = jnp.where(head_mask(g, h, hd), mixed[h * tiles:(h + 1) * tiles], together)
        parts.append(together)
    for g in range(0, groups, 2):
        a, b = parts[g], parts[g + 1]
        lanes = [a[:, :128], a[:, 128:] + b[:, :128], b[:, 128:]]
        attended = jnp.concatenate(lanes, axis=1).astype(BF16)
        out_ref[:, pl.ds(g // 2 * 384, 384)] = attended

    pl.when(has_left)(to_left.wait_send)
    pl.when(has_right)(to_right.wait_send)
    pl.when(has_up)(to_up.wait_send)
    pl.when(has_down)(to_down.wait_send)
    pl.when(has_left & has_up)(left_to_up.wait_send)
    pl.when(has_left & has_down)(left_to_down.wait_send)
    pl.when(has_right & has_up)(right_to_up.wait_send)
    pl.when(has_right & has_down)(right_to_down.wait_send)
    for copy in dil:
        copy.wait_send()


def solution(mesh):
    n_row, n_col = mesh.shape["row"], mesh.shape["col"]

    def per_device(q, k, v, tissue, dilation_levels, segment_levels, output_matrix):
        dr, dc, width = q.shape
        tiles = dr * dc
        sel = tiles // DILATION_MIN
        groups = HEAD_COUNT // HEADS_TOGETHER
        stacked = HEADS_TOGETHER * tiles
        any_space = pl.BlockSpec(memory_space=pl.ANY)
        vmem = pl.BlockSpec(memory_space=pltpu.VMEM)
        smem = pl.BlockSpec(memory_space=pltpu.SMEM)
        out = pl.pallas_call(
            functools.partial(kernel, n_row, n_col, dr, dc),
            out_shape=jax.ShapeDtypeStruct((tiles, width), BF16),
            in_specs=[any_space, any_space, any_space, vmem, smem, smem],
            out_specs=vmem,
            scratch_shapes=[
                pltpu.VMEM((tiles, width), BF16),
                pltpu.VMEM((2, tiles, width), BF16),
                pltpu.VMEM((2, 3 * tiles, width), BF16),
                pltpu.VMEM((2, 2 * tiles + sel * n_col, width), BF16),
                pltpu.VMEM((2, tiles, width), BF16),
                pltpu.VMEM((2, sel, width), BF16),
                pltpu.VMEM((tiles, tiles), F32),
                pltpu.VMEM((tiles, 3 * tiles), F32),
                pltpu.VMEM((HEAD_COUNT, tiles, 2 * tiles + sel * n_col), F32),
                pltpu.VMEM((groups, stacked, 256), F32),
                pltpu.VMEM((groups, stacked, 1), F32),
                pltpu.VMEM((groups, stacked, 1), F32),
                pltpu.SemaphoreType.DMA((3,)),
                pltpu.SemaphoreType.DMA((8,)),
                pltpu.SemaphoreType.DMA((8,)),
                pltpu.SemaphoreType.DMA((n_col,)),
                pltpu.SemaphoreType.DMA((n_col,)),
            ],
            compiler_params=pltpu.CompilerParams(
                collective_id=0, has_side_effects=True, vmem_limit_bytes=40 * 1024 * 1024
            ),
        )(
            q.reshape(tiles, width), k.reshape(tiles, width), v.reshape(tiles, width),
            tissue, dilation_levels, segment_levels,
        )
        encoded = jnp.dot(out, output_matrix, preferred_element_type=F32).astype(BF16)
        return encoded.reshape(dr, dc, width)

    split = P("row", "col", None)
    return jax.shard_map(
        per_device,
        mesh=mesh,
        in_specs=(split, split, split, P(), P(), P(), P()),
        out_specs=split,
        check_vma=False,
    )
```

time: 32.7 us -> 38.3 us (1.17)
  local copies, waits for them, and re-layouts: 1.62 us -> 4.91 us
  Pallas kernels: 30.8 us -> 32.1 us
  matrix products: 0 us -> 1.02 us
    unnamed x1 -> x14, local copies, waits for them, and re-layouts: 1.62 us -> 4.91 us
    pallas_call x1, Pallas kernels: 30.8 us -> 32.1 us  [per_device(): pl.pallas_call(functools.partial(kernel, n_row, n_col, dr, dc), out_shape...]
    dot_general x0 -> x1, matrix products: none -> 1.02 us  [per_device(): jnp.dot(out, output_matrix, preferred_element_type=F32).astype(BF16)]
where the time goes in v2:
time: 38.3 us; the launch traced here: 38 us
  Pallas kernels  32.1 us (84%)
  local copies, waits for them, and re-layouts  4.91 us (13%)
  matrix products  1.02 us (3%)
    pallas_call x1, Pallas kernels, per_device(): pl.pallas_call(functools.partial(kernel, n_row, n_col, dr, dc), out_shape...  32.1 us
    unnamed x14, local copies, waits for them, and re-layouts  4.91 us
    dot_general x1, matrix products, per_device(): jnp.dot(out, output_matrix, preferred_element_type=F32).astype(BF16)  1.02 us

profile of v2, /device:TPU:3, one launch (start us, length us, event | category | flops | bytes accessed | tf_op | source)
XLA Modules:
  0.0 38.0 jit_solution(9093122700866340453)
XLA Ops:
  0.0 0.0 copy-start
  0.0 0.0 copy-start.1
  0.0 1.0 %copy-done.1 = bf16[8,16,768]{2,1,0:T(8,128)(2,1)S(1)} copy-done((bf16[8,16,768]{2,1,0:T(8,128)(2,1)S(1)}, bf16[8,16,768]{2,1,0:T(8,128)(2,1)}, u32[]{:S(2)}) %copy-start.1) | copy-done | bytes 196632
  1.0 0.0 copy-start.2
  1.0 0.9 %copy-done.2 = bf16[8,16,768]{2,1,0:T(8,128)(2,1)S(1)} copy-done((bf16[8,16,768]{2,1,0:T(8,128)(2,1)S(1)}, bf16[8,16,768]{2,1,0:T(8,128)(2,1)}, u32[]{:S(2)}) %copy-start.2) | copy-done | bytes 196632
  2.0 0.0 copy-start.3
  2.0 0.9 %copy-done.3 = bf16[8,16,768]{2,1,0:T(8,128)(2,1)S(1)} copy-done((bf16[8,16,768]{2,1,0:T(8,128)(2,1)S(1)}, bf16[8,16,768]{2,1,0:T(8,128)(2,1)}, u32[]{:S(2)}) %copy-start.3) | copy-done | bytes 196632
  2.9 0.0 copy-start.4
  2.9 0.7 %copy-done.4 = s32[32,128]{1,0:T(8,128)S(1)} copy-done((s32[32,128]{1,0:T(8,128)S(1)}, s32[32,128]{1,0:T(8,128)}, u32[]{:S(2)}) %copy-start.4) | copy-done | bytes 16408
  3.6 0.0 copy-start.5
  3.6 0.7 %copy-done.5 = s32[16]{0:T(128)S(1)} copy-done((s32[16]{0:T(128)S(1)}, s32[16]{0:T(128)}, u32[]{:S(2)}) %copy-start.5) | copy-done | bytes 88
  4.3 0.0 copy-start.6
  4.3 0.7 %copy-done.6 = s32[16]{0:T(128)S(1)} copy-done((s32[16]{0:T(128)S(1)}, s32[16]{0:T(128)}, u32[]{:S(2)}) %copy-start.6) | copy-done | bytes 88
  4.9 32.1 %shard_map.73 = bf16[128,768]{1,0:T(8,128)(2,1)S(1)} custom-call(bf16[128,768]{1,0:T(8,128)(2,1)S(1)} %bitcast.6, bf16[128,768]{1,0:T(8,128)(2,1)S(1)} %bitcast.7, bf16[128,768]{1,0:T(8,128)(2,1)S(1)} %bitcast.8, s32[32,128]{1,0:T(8,128)S(1)} %copy-done.4, s32[16]{0:T(128)S(1)} %copy-done.5, s32[16]{0:T(128)S(1)} %copy-done.6), custom_call_target="tpu_custom_call" | custom-call | tf_op jit(solution)/shard_map/pallas_call | solution.py:327
  37.0 0.0 copy-done
  37.0 1.0 %convolution_convert_fusion = bf16[128,768]{1,0:T(8,128)(2,1)} fusion(bf16[128,768]{1,0:T(8,128)(2,1)S(1)} %shard_map.73, bf16[768,768]{1,0:T(8,128)(2,1)S(1)} %copy-done), kind=kOutput, calls=%fused_computation | convolution fusion | flops 151093248 | bytes 1572864 | tf_op jit(solution)/shard_map/dot_general | solution.py:358
Async XLA Ops:
  0.0 37.0 %copy-start = (bf16[768,768]{1,0:T(8,128)(2,1)S(1)}, bf16[768,768]{1,0:T(8,128)(2,1)}, u32[]{:S(2)}) copy-start(bf16[768,768]{1,0:T(8,128)(2,1)} %param.13) | copy-start | bytes 3538948
  0.0 1.0 %copy-start.1 = (bf16[8,16,768]{2,1,0:T(8,128)(2,1)S(1)}, bf16[8,16,768]{2,1,0:T(8,128)(2,1)}, u32[]{:S(2)}) copy-start(bf16[8,16,768]{2,1,0:T(8,128)(2,1)} %param.7) | copy-start | bytes 589828
  1.0 0.9 %copy-start.2 = (bf16[8,16,768]{2,1,0:T(8,128)(2,1)S(1)}, bf16[8,16,768]{2,1,0:T(8,128)(2,1)}, u32[]{:S(2)}) copy-start(bf16[8,16,768]{2,1,0:T(8,128)(2,1)} %param.8) | copy-start | bytes 589828
  2.0 0.9 %copy-start.3 = (bf16[8,16,768]{2,1,0:T(8,128)(2,1)S(1)}, bf16[8,16,768]{2,1,0:T(8,128)(2,1)}, u32[]{:S(2)}) copy-start(bf16[8,16,768]{2,1,0:T(8,128)(2,1)} %param.9) | copy-start | bytes 589828
  2.9 0.7 %copy-start.4 = (s32[32,128]{1,0:T(8,128)S(1)}, s32[32,128]{1,0:T(8,128)}, u32[]{:S(2)}) copy-start(s32[32,128]{1,0:T(8,128)} %tissue_ref.1) | copy-start | bytes 49156
  3.6 0.7 %copy-start.5 = (s32[16]{0:T(128)S(1)}, s32[16]{0:T(128)}, u32[]{:S(2)}) copy-start(s32[16]{0:T(128)} %dil_ref.1) | copy-start | bytes 196
  4.3 0.7 %copy-start.6 = (s32[16]{0:T(128)S(1)}, s32[16]{0:T(128)}, u32[]{:S(2)}) copy-start(s32[16]{0:T(128)} %seg_ref.1) | copy-start | bytes 196

commit v3 on v2

--- a/solution.py
+++ b/solution.py
@@ -37,21 +37,25 @@
     return (lane >= 0) & (lane < head_dimension)
 
 
-def gathered_tissue(tissue, key_rows, key_cols):
+def gathered_tissue(tissue, n, key_row, key_col, lanes):
     rows, cols = tissue.shape
-    n = key_rows.shape[1]
-    pick = one_hot(iota((cols, n), 0) == key_cols)
-    by_col = jnp.dot(tissue, pick, preferred_element_type=F32)
-    keep = iota((rows, n), 0) == key_rows
-    return jnp.sum(jnp.where(keep, by_col, 0.0), axis=0, keepdims=True)
-
-
-def window_bias(tissue, key_rel_row, key_rel_col, row_offset, column_offset, dr, dc):
-    present = gathered_tissue(tissue, key_rel_row + row_offset, key_rel_col + column_offset)
-    n = key_rel_row.shape[1]
-    q = iota((dr * dc, n), 0)
-    row_gap = jnp.abs(key_rel_row - q // dc)
-    col_gap = jnp.abs(key_rel_col - q % dc)
+    pick = one_hot(iota((n, cols), 1) == key_col(iota((n, cols), 0)))
+    by_col = lax.dot_general(
+        pick, tissue, (((1,), (1,)), ((), ())), preferred_element_type=F32
+    )
+    keep = iota((n, rows), 1) == key_row(iota((n, rows), 0))
+    kept = jnp.where(keep, by_col, 0.0).astype(BF16)
+    return jnp.dot(kept, jnp.ones((rows, lanes), BF16), preferred_element_type=F32)
+
+
+def window_bias(tissue, n, key_row, key_col, row_offset, column_offset, dr, dc):
+    present = gathered_tissue(
+        tissue, n, lambda k: key_row(k) + row_offset, lambda k: key_col(k) + column_offset,
+        dr * dc,
+    )
+    k, q = iota((n, dr * dc), 0), iota((n, dr * dc), 1)
+    row_gap = jnp.abs(key_row(k) - q // dc)
+    col_gap = jnp.abs(key_col(k) - q % dc)
     near = (row_gap <= R) & (col_gap <= R) & (present > 0.5)
     self_key = (row_gap + col_gap) == 0
     return jnp.where(near | self_key, 0.0, NEG_FILL)
@@ -60,7 +64,7 @@
 def kernel(
     n_row, n_col, dr, dc,
     q_hbm, k_hbm, v_hbm, tissue_ref, dil_ref, seg_ref, out_ref,
-    q_ref, own_kv, mid_kv, far_kv, halves, chosen, bias_own, bias_mid, bias_far,
+    q_ref, query, own_kv, mid_kv, far_kv, halves, chosen, bias_own, bias_mid, bias_far,
     numer, highest, total, local_sem, send_sem, recv_sem, dil_send, dil_recv,
 ):
     row, col = lax.axis_index("row"), lax.axis_index("col")
@@ -178,56 +182,63 @@
     tissue = tissue_ref[...].astype(F32).astype(BF16)
     row_offset, column_offset = row * dr, col * dc
 
-    def bias(key_row, key_col):
-        return window_bias(tissue, key_row, key_col, row_offset, column_offset, dr, dc)
+    def bias(n, key_row, key_col):
+        return window_bias(tissue, n, key_row, key_col, row_offset, column_offset, dr, dc)
 
     def half_col(k):
         return jnp.where(k % tiles >= half, dc, -R) + k % R
 
-    k = iota((1, tiles), 1)
-    bias_own[...] = bias(k // dc, k % dc)
+    bias_own[...] = bias(tiles, lambda k: k // dc, lambda k: k % dc)
     for block, shift in ((0, -dr), (1, dr)):
-        bias_mid[:, pl.ds(block * tiles, tiles)] = bias(k // dc + shift, k % dc)
-    bias_mid[:, pl.ds(2 * tiles, tiles)] = bias(k % half // R, half_col(k))
+        bias_mid[pl.ds(block * tiles, tiles)] = bias(
+            tiles, lambda k: k // dc + shift, lambda k: k % dc
+        )
+    bias_mid[pl.ds(2 * tiles, tiles)] = bias(tiles, lambda k: k % half // R, half_col)
 
     factor = math.log2(math.e) / math.sqrt(hd)
     groups = HEAD_COUNT // HEADS_TOGETHER
-    stacked = HEADS_TOGETHER * tiles
-
-    def attend(g, kv, extra, before):
-        base, _ = lane_window(g, hd)
-        query = q_ref[:, pl.ds(base, 256)]
-        query = jnp.concatenate(
-            [
-                jnp.where(head_mask(g, h, hd), query, jnp.zeros_like(query))
-                for h in range(HEADS_TOGETHER)
-            ],
-            axis=0,
-        )
-        scores = lax.dot_general(
-            query, kv[0, :, pl.ds(base, 256)], (((1,), (1,)), ((), ())),
-            preferred_element_type=F32,
-        )
-        scores = scores.reshape(HEADS_TOGETHER, tiles, kv.shape[1]) + extra
-        scores = scores.reshape(stacked, kv.shape[1])
-        top = jnp.max(scores, axis=-1, keepdims=True)
-        if before is not None:
-            old_numer, old_top, old_total = before
-            top = jnp.maximum(top, old_top)
-        probs = jnp.exp2((scores - top) * factor)
-        new_total = jnp.sum(probs, axis=-1, keepdims=True)
-        new_numer = jnp.dot(
-            probs.astype(BF16), kv[1, :, pl.ds(base, 256)], preferred_element_type=F32
-        )
-        if before is not None:
-            keep = jnp.exp2((old_top - top) * factor)
-            new_total += keep * old_total
-            new_numer += keep * old_numer
-        return new_numer, top, new_total
-
     loads[2].wait()
     for g in range(groups):
-        numer[g], highest[g], total[g] = attend(g, own_kv, bias_own[...][None], None)
+        base, _ = lane_window(g, hd)
+        lanes = q_ref[:, pl.ds(base, 256)]
+        for h in range(HEADS_TOGETHER):
+            query[g, pl.ds(h * tiles, tiles)] = jnp.where(
+                head_mask(g, h, hd), lanes, jnp.zeros_like(lanes)
+            )
+
+    def attend(kv, extra, first, last):
+        values = kv[1].T
+        finished = []
+        for g in range(groups):
+            base, _ = lane_window(g, hd)
+            scores = lax.dot_general(
+                kv[0, :, pl.ds(base, 256)], query[g], (((1,), (1,)), ((), ())),
+                preferred_element_type=F32,
+            )
+            for h in range(HEADS_TOGETHER):
+                head = g * HEADS_TOGETHER + h
+                part = scores[:, h * tiles:(h + 1) * tiles] + extra(head)
+                top = jnp.max(part, axis=0, keepdims=True)
+                if not first:
+                    old_top = highest[head]
+                    top = jnp.maximum(top, old_top)
+                probs = jnp.exp2((part - top) * factor)
+                new_total = jnp.sum(probs, axis=0, keepdims=True)
+                new_numer = jnp.dot(
+                    values[head * hd:(head + 1) * hd], probs.astype(BF16),
+                    preferred_element_type=F32,
+                )
+                if not first:
+                    keep = jnp.exp2((old_top - top) * factor)
+                    new_total += keep * total[head]
+                    new_numer += keep * numer[head]
+                if last:
+                    finished.append(new_numer * (1.0 / new_total))
+                else:
+                    highest[head], total[head], numer[head] = top, new_total, new_numer
+        return finished
+
+    attend(own_kv, lambda head: bias_own[...], True, False)
 
     @pl.when(has_left)
     def _():
@@ -242,33 +253,36 @@
         pl.when(has_down)(right_to_down.start)
 
     for block, shift in ((0, -dr), (1, dr)):
-        bias_far[0, :, pl.ds(block * tiles, tiles)] = bias(k % half // R + shift, half_col(k))
-    for h in range(1, HEAD_COUNT):
-        bias_far[h, :, pl.ds(0, corners)] = bias_far[0, :, pl.ds(0, corners)]
+        shared = bias(tiles, lambda k: k % half // R + shift, half_col)
+        for h in range(HEAD_COUNT):
+            bias_far[h, pl.ds(block * tiles, tiles)] = shared
     n_dil = sel * n_col
-    kd = iota((1, n_dil), 1)
-    dil_row = kd % sel // local_sel
-    dil_col = kd // sel * dc + kd % local_sel * DILATION_MIN
-    q_idx = iota((tiles, n_dil), 0)
-    q_col = column_offset + q_idx % dc
-    same_row = dil_row == q_idx // dc
+
+    def dil_row(k):
+        return k % sel // local_sel
+
+    def dil_col(k):
+        return k // sel * dc + k % local_sel * DILATION_MIN
+
+    k, q = iota((n_dil, tiles), 0), iota((n_dil, tiles), 1)
+    same_row = dil_row(k) == q // dc
     for p in range(DILATION_MIN):
-        key_col = dil_col + p
-        present = gathered_tissue(tissue, dil_row + row_offset, key_col) > 0.5
-        apart = key_col ^ q_col
+        present = gathered_tissue(
+            tissue, n_dil, lambda k: dil_row(k) + row_offset, lambda k: dil_col(k) + p, tiles
+        )
+        allowed = same_row & (present > 0.5)
+        key_col = dil_col(k) + p
+        apart = key_col ^ (column_offset + q % dc)
         for head in range(p, HEAD_COUNT, DILATION_MIN):
             stride = jnp.left_shift(jnp.int32(DILATION_MIN), dil_ref[head])
             segment = jnp.right_shift(jnp.int32(dc * n_col), seg_ref[head])
-            key_ok = present & ((key_col & (stride - 1)) == (head & (stride - 1)))
-            ok = key_ok & same_row & (apart < segment)
-            bias_far[head, :, pl.ds(corners, n_dil)] = jnp.where(ok, 0.0, NEG_FILL)
+            phase_ok = ((key_col ^ head) & (stride - 1)) == 0
+            ok = allowed & phase_ok & (apart < segment)
+            bias_far[head, pl.ds(corners, n_dil)] = jnp.where(ok, 0.0, NEG_FILL)
 
     pl.when(has_down)(to_up.wait_recv)
     pl.when(has_up)(to_down.wait_recv)
-    for g in range(groups):
-        numer[g], highest[g], total[g] = attend(
-            g, mid_kv, bias_mid[...][None], (numer[g], highest[g], total[g])
-        )
+    attend(mid_kv, lambda head: bias_mid[...], False, False)
 
     for copy in dil:
         copy.wait_recv()
@@ -283,22 +297,8 @@
         pl.when(has_up)(right_to_down.wait_recv)
         pl.when(has_down)(right_to_up.wait_recv)
 
-    parts = []
-    for g in range(groups):
-        heads = pl.ds(g * HEADS_TOGETHER, HEADS_TOGETHER)
-        top_numer, _, top_total = attend(
-            g, far_kv, bias_far[heads], (numer[g], highest[g], total[g])
-        )
-        mixed = top_numer * (1.0 / top_total)
-        together = jnp.zeros((tiles, 256), F32)
-        for h in range(HEADS_TOGETHER):
-            together = jnp.where(head_mask(g, h, hd), mixed[h * tiles:(h + 1) * tiles], together)
-        parts.append(together)
-    for g in range(0, groups, 2):
-        a, b = parts[g], parts[g + 1]
-        lanes = [a[:, :128], a[:, 128:] + b[:, :128], b[:, 128:]]
-        attended = jnp.concatenate(lanes, axis=1).astype(BF16)
-        out_ref[:, pl.ds(g // 2 * 384, 384)] = attended
+    finished = attend(far_kv, lambda head: bias_far[head], False, True)
+    out_ref[...] = jnp.concatenate(finished, axis=0).T.astype(BF16)
 
     pl.when(has_left)(to_left.wait_send)
     pl.when(has_right)(to_right.wait_send)
@@ -320,7 +320,6 @@
         tiles = dr * dc
         sel = tiles // DILATION_MIN
         groups = HEAD_COUNT // HEADS_TOGETHER
-        stacked = HEADS_TOGETHER * tiles
         any_space = pl.BlockSpec(memory_space=pl.ANY)
         vmem = pl.BlockSpec(memory_space=pltpu.VMEM)
         smem = pl.BlockSpec(memory_space=pltpu.SMEM)
@@ -331,17 +330,18 @@
             out_specs=vmem,
             scratch_shapes=[
                 pltpu.VMEM((tiles, width), BF16),
+                pltpu.VMEM((groups, HEADS_TOGETHER * tiles, 256), BF16),
                 pltpu.VMEM((2, tiles, width), BF16),
                 pltpu.VMEM((2, 3 * tiles, width), BF16),
                 pltpu.VMEM((2, 2 * tiles + sel * n_col, width), BF16),
                 pltpu.VMEM((2, tiles, width), BF16),
                 pltpu.VMEM((2, sel, width), BF16),
                 pltpu.VMEM((tiles, tiles), F32),
-                pltpu.VMEM((tiles, 3 * tiles), F32),
-                pltpu.VMEM((HEAD_COUNT, tiles, 2 * tiles + sel * n_col), F32),
-                pltpu.VMEM((groups, stacked, 256), F32),
-                pltpu.VMEM((groups, stacked, 1), F32),
-                pltpu.VMEM((groups, stacked, 1), F32),
+                pltpu.VMEM((3 * tiles, tiles), F32),
+                pltpu.VMEM((HEAD_COUNT, 2 * tiles + sel * n_col, tiles), F32),
+                pltpu.VMEM((HEAD_COUNT, width // HEAD_COUNT, tiles), F32),
+                pltpu.VMEM((HEAD_COUNT, 1, tiles), F32),
+                pltpu.VMEM((HEAD_COUNT, 1, tiles), F32),
                 pltpu.SemaphoreType.DMA((3,)),
                 pltpu.SemaphoreType.DMA((8,)),
                 pltpu.SemaphoreType.DMA((8,)),
@@ -349,7 +349,7 @@
                 pltpu.SemaphoreType.DMA((n_col,)),
             ],
             compiler_params=pltpu.CompilerParams(
-                collective_id=0, has_side_effects=True, vmem_limit_bytes=40 * 1024 * 1024
+                collective_id=0, has_side_effects=True, vmem_limit_bytes=56 * 1024 * 1024
             ),
         )(
             q.reshape(tiles, width), k.reshape(tiles, width), v.reshape(tiles, width),

time: 38.3 us -> 30 us (0.78)
  local copies, waits for them, and re-layouts: 4.91 us -> 0.01 us
  Pallas kernels: 32.1 us -> 27.9 us
  matrix products: 1.02 us -> 1.93 us
    unnamed x14 -> x2, local copies, waits for them, and re-layouts: 4.91 us -> 0.01 us
    pallas_call x1, Pallas kernels: 32.1 us -> 27.9 us  [per_device(): pl.pallas_call(functools.partial(kernel, n_row, n_col, dr, dc), out_shape...]
    dot_general x1, matrix products: 1.02 us -> 1.93 us  [per_device(): jnp.dot(out, output_matrix, preferred_element_type=F32).astype(BF16)]
where the time goes in v3:
time: 30 us; the launch traced here: 29.8 us
  Pallas kernels  27.9 us (93%)
  matrix products  1.93 us (6%)
    pallas_call x1, Pallas kernels, per_device(): pl.pallas_call(functools.partial(kernel, n_row, n_col, dr, dc), out_shape...  27.9 us
    dot_general x1, matrix products, per_device(): jnp.dot(out, output_matrix, preferred_element_type=F32).astype(BF16)  1.93 us

profile of v3, /device:TPU:3, one launch (start us, length us, event | category | flops | bytes accessed | tf_op | source)
XLA Modules:
  0.0 29.8 jit_solution(7910071708235577549)
XLA Ops:
  0.0 0.0 copy-start
  0.0 27.9 %shard_map.73 = bf16[128,768]{1,0:T(8,128)(2,1)} custom-call(bf16[128,768]{1,0:T(8,128)(2,1)} %bitcast.6, bf16[128,768]{1,0:T(8,128)(2,1)} %bitcast.7, bf16[128,768]{1,0:T(8,128)(2,1)} %bitcast.8, s32[32,128]{1,0:T(8,128)} %tissue_ref.1, s32[16]{0:T(128)} %dil_ref.1, s32[16]{0:T(128)} %seg_ref.1), custom_call_target="tpu_custom_call" | custom-call | tf_op jit(solution)/shard_map/pallas_call | solution.py:326
  27.9 0.0 copy-done
  27.9 1.9 %convolution_convert_fusion = bf16[128,768]{1,0:T(8,128)(2,1)} fusion(bf16[128,768]{1,0:T(8,128)(2,1)} %shard_map.73, bf16[768,768]{1,0:T(8,128)(2,1)S(1)} %copy-done), kind=kOutput, calls=%fused_computation | convolution fusion | flops 151093248 | bytes 1572864 | tf_op jit(solution)/shard_map/dot_general | solution.py:358
Async XLA Ops:
  0.0 27.9 %copy-start = (bf16[768,768]{1,0:T(8,128)(2,1)S(1)}, bf16[768,768]{1,0:T(8,128)(2,1)}, u32[]{:S(2)}) copy-start(bf16[768,768]{1,0:T(8,128)(2,1)} %param.13) | copy-start | bytes 3538948

commit v4 on v3

--- a/solution.py
+++ b/solution.py
@@ -99,8 +99,17 @@
     def _():
         pl.semaphore_signal(barrier, inc=1, device_id=down, device_id_type=MESH)
 
-    for d in range(1, n_col):
-        peer = (row, lax.rem(col + d, n_col))
+    @pl.when(has_left)
+    def _():
+        pl.semaphore_signal(barrier, inc=1, device_id=left, device_id_type=MESH)
+
+    @pl.when(has_right)
+    def _():
+        pl.semaphore_signal(barrier, inc=1, device_id=right, device_id_type=MESH)
+
+    partner = (row, col + 1 - 2 * (col % 2))
+    same_parity = [(row, lax.rem(col + 2 * d, n_col)) for d in range(1, n_col // 2)]
+    for peer in same_parity:
         pl.semaphore_signal(barrier, inc=1, device_id=peer, device_id_type=MESH)
 
     def remote(src, dst, kind, device):
@@ -112,18 +121,22 @@
     def mid(first, count):
         return mid_kv.at[:, pl.ds(first, count)]
 
-    def corner(index):
-        return far_kv.at[:, pl.ds(index * half, half)]
-
-    left_here, right_here = mid(2 * tiles, half), mid(2 * tiles + half, half)
     to_up = remote(own_kv, mid(tiles, tiles), 0, up)
     to_down = remote(own_kv, mid(0, tiles), 1, down)
-    to_left = remote(halves.at[:, pl.ds(0, half)], right_here, 2, left)
-    to_right = remote(halves.at[:, pl.ds(half, half)], left_here, 3, right)
-    left_to_up = remote(left_here, corner(2), 4, up)
-    left_to_down = remote(left_here, corner(0), 5, down)
-    right_to_up = remote(right_here, corner(3), 6, up)
-    right_to_down = remote(right_here, corner(1), 7, down)
+    to_left, to_right, left_to_up, left_to_down, right_to_up, right_to_down = (
+        [], [], [], [], [], []
+    )
+    for t in range(2):
+        left_here = mid_kv.at[t, pl.ds(2 * tiles, half)]
+        right_here = mid_kv.at[t, pl.ds(2 * tiles + half, half)]
+        corner = [far_kv.at[t, pl.ds(index * half, half)] for index in range(4)]
+        sem = 2 + 6 * t
+        to_left.append(remote(halves.at[t, pl.ds(0, half)], right_here, sem, left))
+        to_right.append(remote(halves.at[t, pl.ds(half, half)], left_here, sem + 1, right))
+        left_to_up.append(remote(left_here, corner[2], sem + 2, up))
+        left_to_down.append(remote(left_here, corner[0], sem + 3, down))
+        right_to_up.append(remote(right_here, corner[3], sem + 4, up))
+        right_to_down.append(remote(right_here, corner[1], sem + 5, down))
 
     i, j = iota((tiles, tiles), 0), iota((tiles, tiles), 1)
     within = i % half
@@ -132,7 +145,10 @@
     s = i % sel
     phase_order = one_hot(j == s // local_sel * dc + s % local_sel * DILATION_MIN + i // sel)
     lane_phase = iota((1, width), 1) // hd % DILATION_MIN
-    slot = pl.ds(pl.multiple_of(corners + col * sel, sel), sel)
+    pairs = n_col // 2
+    own_slot = col % 2 * pairs + col // 2
+    slot = pl.ds(pl.multiple_of(corners + own_slot * sel, sel), sel)
+    parity_slots = pl.ds(pl.multiple_of(corners + col % 2 * pairs * sel, sel), pairs * sel)
 
     loads[0].wait()
     loads[1].wait()
@@ -140,10 +156,13 @@
         halves[t] = jnp.dot(split_order, own_kv[t], preferred_element_type=F32).astype(BF16)
     pl.semaphore_wait(
         barrier,
-        (n_col - 1) + jnp.where(has_up, 1, 0) + jnp.where(has_down, 1, 0),
-    )
-    pl.when(has_left)(to_left.start)
-    pl.when(has_right)(to_right.start)
+        len(same_parity)
+        + jnp.where(has_up, 1, 0) + jnp.where(has_down, 1, 0)
+        + jnp.where(has_left, 1, 0) + jnp.where(has_right, 1, 0),
+    )
+    for t in range(2):
+        pl.when(has_left)(to_left[t].start)
+        pl.when(has_right)(to_right[t].start)
     pl.when(has_up)(to_up.start)
     pl.when(has_down)(to_down.start)
     for t in range(2):
@@ -155,14 +174,19 @@
         chosen[t] = picked
         far_kv[t, slot] = picked
     dil = []
-    for d in range(1, n_col):
+    for d, peer in enumerate(same_parity):
         copy = pltpu.make_async_remote_copy(
             src_ref=chosen, dst_ref=far_kv.at[:, slot],
             send_sem=dil_send.at[d], recv_sem=dil_recv.at[d],
-            device_id=(row, lax.rem(col + d, n_col)), device_id_type=MESH,
+            device_id=peer, device_id_type=MESH,
         )
         copy.start()
         dil.append(copy)
+    to_partner = pltpu.make_async_remote_copy(
+        src_ref=far_kv.at[:, parity_slots], dst_ref=far_kv.at[:, parity_slots],
+        send_sem=dil_send.at[pairs], recv_sem=dil_recv.at[pairs],
+        device_id=partner, device_id_type=MESH,
+    )
 
     def clear(ref, first, count):
         ref[:, pl.ds(first, count)] = jnp.zeros((2, count, width), BF16)
@@ -240,17 +264,23 @@
 
     attend(own_kv, lambda head: bias_own[...], True, False)
 
-    @pl.when(has_left)
-    def _():
-        to_right.wait_recv()
-        pl.when(has_up)(left_to_up.start)
-        pl.when(has_down)(left_to_down.start)
-
-    @pl.when(has_right)
-    def _():
-        to_left.wait_recv()
-        pl.when(has_up)(right_to_up.start)
-        pl.when(has_down)(right_to_down.start)
+    for t in range(2):
+
+        @pl.when(has_left)
+        def _(t=t):
+            to_right[t].wait_recv()
+            pl.when(has_up)(left_to_up[t].start)
+            pl.when(has_down)(left_to_down[t].start)
+
+        @pl.when(has_right)
+        def _(t=t):
+            to_left[t].wait_recv()
+            pl.when(has_up)(right_to_up[t].start)
+            pl.when(has_down)(right_to_down[t].start)
+
+    for copy in dil:
+        copy.wait_recv()
+    to_partner.start()
 
     for block, shift in ((0, -dr), (1, dr)):
         shared = bias(tiles, lambda k: k % half // R + shift, half_col)
@@ -262,7 +292,9 @@
         return k % sel // local_sel
 
     def dil_col(k):
-        return k // sel * dc + k % local_sel * DILATION_MIN
+        place = k // sel
+        device = place % pairs * 2 + place // pairs
+        return device * dc + k % local_sel * DILATION_MIN
 
     k, q = iota((n_dil, tiles), 0), iota((n_dil, tiles), 1)
     same_row = dil_row(k) == q // dc
@@ -284,32 +316,28 @@
     pl.when(has_up)(to_down.wait_recv)
     attend(mid_kv, lambda head: bias_mid[...], False, False)
 
-    for copy in dil:
-        copy.wait_recv()
-
-    @pl.when(has_left)
-    def _():
-        pl.when(has_up)(left_to_down.wait_recv)
-        pl.when(has_down)(left_to_up.wait_recv)
-
-    @pl.when(has_right)
-    def _():
-        pl.when(has_up)(right_to_down.wait_recv)
-        pl.when(has_down)(right_to_up.wait_recv)
+    to_partner.wait_recv()
+    for t in range(2):
+        pl.when(has_left & has_up)(left_to_down[t].wait_recv)
+        pl.when(has_left & has_down)(left_to_up[t].wait_recv)
+        pl.when(has_right & has_up)(right_to_down[t].wait_recv)
+        pl.when(has_right & has_down)(right_to_up[t].wait_recv)
 
     finished = attend(far_kv, lambda head: bias_far[head], False, True)
     out_ref[...] = jnp.concatenate(finished, axis=0).T.astype(BF16)
 
-    pl.when(has_left)(to_left.wait_send)
-    pl.when(has_right)(to_right.wait_send)
     pl.when(has_up)(to_up.wait_send)
     pl.when(has_down)(to_down.wait_send)
-    pl.when(has_left & has_up)(left_to_up.wait_send)
-    pl.when(has_left & has_down)(left_to_down.wait_send)
-    pl.when(has_right & has_up)(right_to_up.wait_send)
-    pl.when(has_right & has_down)(right_to_down.wait_send)
+    for t in range(2):
+        pl.when(has_left)(to_left[t].wait_send)
+        pl.when(has_right)(to_right[t].wait_send)
+        pl.when(has_left & has_up)(left_to_up[t].wait_send)
+        pl.when(has_left & has_down)(left_to_down[t].wait_send)
+        pl.when(has_right & has_up)(right_to_up[t].wait_send)
+        pl.when(has_right & has_down)(right_to_down[t].wait_send)
     for copy in dil:
         copy.wait_send()
+    to_partner.wait_send()
 
 
 def solution(mesh):
@@ -320,13 +348,13 @@
         tiles = dr * dc
         sel = tiles // DILATION_MIN
         groups = HEAD_COUNT // HEADS_TOGETHER
-        any_space = pl.BlockSpec(memory_space=pl.ANY)
+        hbm = pl.BlockSpec(memory_space=pltpu.HBM)
         vmem = pl.BlockSpec(memory_space=pltpu.VMEM)
         smem = pl.BlockSpec(memory_space=pltpu.SMEM)
         out = pl.pallas_call(
             functools.partial(kernel, n_row, n_col, dr, dc),
             out_shape=jax.ShapeDtypeStruct((tiles, width), BF16),
-            in_specs=[any_space, any_space, any_space, vmem, smem, smem],
+            in_specs=[hbm, hbm, hbm, vmem, smem, smem],
             out_specs=vmem,
             scratch_shapes=[
                 pltpu.VMEM((tiles, width), BF16),
@@ -343,8 +371,8 @@
                 pltpu.VMEM((HEAD_COUNT, 1, tiles), F32),
                 pltpu.VMEM((HEAD_COUNT, 1, tiles), F32),
                 pltpu.SemaphoreType.DMA((3,)),
-                pltpu.SemaphoreType.DMA((8,)),
-                pltpu.SemaphoreType.DMA((8,)),
+                pltpu.SemaphoreType.DMA((14,)),
+                pltpu.SemaphoreType.DMA((14,)),
                 pltpu.SemaphoreType.DMA((n_col,)),
                 pltpu.SemaphoreType.DMA((n_col,)),
             ],

time: 30 us -> 27.3 us (0.910)
  the two profiles are of different devices: /device:TPU:3 before, /device:TPU:0 now
where the time goes in v4:
time: 27.3 us; the launch traced here: 27.1 us
  Pallas kernels  25.1 us (92%)
  matrix products  1.93 us (7%)
    pallas_call x1, Pallas kernels, per_device(): pl.pallas_call(functools.partial(kernel, n_row, n_col, dr, dc), out_shape...  25.1 us
    dot_general x1, matrix products, per_device(): jnp.dot(out, output_matrix, preferred_element_type=F32).astype(BF16)  1.93 us

profile of v4, /device:TPU:0, one launch (start us, length us, event | category | flops | bytes accessed | tf_op | source)
XLA Modules:
  0.0 27.1 jit_solution(1882422830493122048)
XLA Ops:
  0.0 0.0 copy-start
  0.0 25.1 %shard_map.73 = bf16[128,768]{1,0:T(8,128)(2,1)} custom-call(bf16[128,768]{1,0:T(8,128)(2,1)} %bitcast.6, bf16[128,768]{1,0:T(8,128)(2,1)} %bitcast.7, bf16[128,768]{1,0:T(8,128)(2,1)} %bitcast.8, s32[32,128]{1,0:T(8,128)} %tissue_ref.1, s32[16]{0:T(128)} %dil_ref.1, s32[16]{0:T(128)} %seg_ref.1), custom_call_target="tpu_custom_call" | custom-call | tf_op jit(solution)/shard_map/pallas_call | solution.py:354
  25.1 0.0 copy-done
  25.2 1.9 %convolution_convert_fusion = bf16[128,768]{1,0:T(8,128)(2,1)} fusion(bf16[128,768]{1,0:T(8,128)(2,1)} %shard_map.73, bf16[768,768]{1,0:T(8,128)(2,1)S(1)} %copy-done), kind=kOutput, calls=%fused_computation | convolution fusion | flops 151093248 | bytes 1572864 | tf_op jit(solution)/shard_map/dot_general | solution.py:386
Async XLA Ops:
  0.0 25.1 %copy-start = (bf16[768,768]{1,0:T(8,128)(2,1)S(1)}, bf16[768,768]{1,0:T(8,128)(2,1)}, u32[]{:S(2)}) copy-start(bf16[768,768]{1,0:T(8,128)(2,1)} %param.13) | copy-start | bytes 3538948

commit v5 on v4

--- a/solution.py
+++ b/solution.py
@@ -230,13 +230,13 @@
                 head_mask(g, h, hd), lanes, jnp.zeros_like(lanes)
             )
 
-    def attend(kv, extra, first, last):
-        values = kv[1].T
+    def attend(kv, begin, count, extra, first, last):
+        values = kv[1, pl.ds(begin, count)].T
         finished = []
         for g in range(groups):
             base, _ = lane_window(g, hd)
             scores = lax.dot_general(
-                kv[0, :, pl.ds(base, 256)], query[g], (((1,), (1,)), ((), ())),
+                kv[0, pl.ds(begin, count), pl.ds(base, 256)], query[g], (((1,), (1,)), ((), ())),
                 preferred_element_type=F32,
             )
             for h in range(HEADS_TOGETHER):
@@ -262,25 +262,7 @@
                     highest[head], total[head], numer[head] = top, new_total, new_numer
         return finished
 
-    attend(own_kv, lambda head: bias_own[...], True, False)
-
-    for t in range(2):
-
-        @pl.when(has_left)
-        def _(t=t):
-            to_right[t].wait_recv()
-            pl.when(has_up)(left_to_up[t].start)
-            pl.when(has_down)(left_to_down[t].start)
-
-        @pl.when(has_right)
-        def _(t=t):
-            to_left[t].wait_recv()
-            pl.when(has_up)(right_to_up[t].start)
-            pl.when(has_down)(right_to_down[t].start)
-
-    for copy in dil:
-        copy.wait_recv()
-    to_partner.start()
+    attend(own_kv, 0, tiles, lambda head: bias_own[...], True, False)
 
     for block, shift in ((0, -dr), (1, dr)):
         shared = bias(tiles, lambda k: k % half // R + shift, half_col)
@@ -314,8 +296,29 @@
 
     pl.when(has_down)(to_up.wait_recv)
     pl.when(has_up)(to_down.wait_recv)
-    attend(mid_kv, lambda head: bias_mid[...], False, False)
-
+    attend(mid_kv, 0, 2 * tiles, lambda head: bias_mid[pl.ds(0, 2 * tiles)], False, False)
+
+    for t in range(2):
+
+        @pl.when(has_left)
+        def _(t=t):
+            to_right[t].wait_recv()
+            pl.when(has_up)(left_to_up[t].start)
+            pl.when(has_down)(left_to_down[t].start)
+
+        @pl.when(has_right)
+        def _(t=t):
+            to_left[t].wait_recv()
+            pl.when(has_up)(right_to_up[t].start)
+            pl.when(has_down)(right_to_down[t].start)
+
+    for copy in dil:
+        copy.wait_recv()
+    to_partner.start()
+
+    attend(
+        mid_kv, 2 * tiles, tiles, lambda head: bias_mid[pl.ds(2 * tiles, tiles)], False, False
+    )
     to_partner.wait_recv()
     for t in range(2):
         pl.when(has_left & has_up)(left_to_down[t].wait_recv)
@@ -323,7 +326,9 @@
         pl.when(has_right & has_up)(right_to_down[t].wait_recv)
         pl.when(has_right & has_down)(right_to_up[t].wait_recv)
 
-    finished = attend(far_kv, lambda head: bias_far[head], False, True)
+    finished = attend(
+        far_kv, 0, corners + n_dil, lambda head: bias_far[head], False, True
+    )
     out_ref[...] = jnp.concatenate(finished, axis=0).T.astype(BF16)
 
     pl.when(has_up)(to_up.wait_send)

time: 27.3 us -> 27.2 us (level)
  no operation moved by 1% of the time
where the time goes in v5:
time: 27.2 us; the launch traced here: 27 us
  Pallas kernels  25.1 us (92%)
  matrix products  1.93 us (7%)
    pallas_call x1, Pallas kernels, per_device(): pl.pallas_call(functools.partial(kernel, n_row, n_col, dr, dc), out_shape...  25.1 us
    dot_general x1, matrix products, per_device(): jnp.dot(out, output_matrix, preferred_element_type=F32).astype(BF16)  1.93 us

profile of v5, /device:TPU:0, one launch (start us, length us, event | category | flops | bytes accessed | tf_op | source)
XLA Modules:
  0.0 27.0 jit_solution(13402214414158757041)
XLA Ops:
  0.0 0.0 copy-start
  0.0 25.1 %shard_map.73 = bf16[128,768]{1,0:T(8,128)(2,1)} custom-call(bf16[128,768]{1,0:T(8,128)(2,1)} %bitcast.6, bf16[128,768]{1,0:T(8,128)(2,1)} %bitcast.7, bf16[128,768]{1,0:T(8,128)(2,1)} %bitcast.8, s32[32,128]{1,0:T(8,128)} %tissue_ref.1, s32[16]{0:T(128)} %dil_ref.1, s32[16]{0:T(128)} %seg_ref.1), custom_call_target="tpu_custom_call" | custom-call | tf_op jit(solution)/shard_map/pallas_call | solution.py:359
  25.1 0.0 copy-done
  25.1 1.9 %convolution_convert_fusion = bf16[128,768]{1,0:T(8,128)(2,1)} fusion(bf16[128,768]{1,0:T(8,128)(2,1)} %shard_map.73, bf16[768,768]{1,0:T(8,128)(2,1)S(1)} %copy-done), kind=kOutput, calls=%fused_computation | convolution fusion | flops 151093248 | bytes 1572864 | tf_op jit(solution)/shard_map/dot_general | solution.py:391
Async XLA Ops:
  0.0 25.1 %copy-start = (bf16[768,768]{1,0:T(8,128)(2,1)S(1)}, bf16[768,768]{1,0:T(8,128)(2,1)}, u32[]{:S(2)}) copy-start(bf16[768,768]{1,0:T(8,128)(2,1)} %param.13) | copy-start | bytes 3538948

commit v6 on v5

--- a/solution.py
+++ b/solution.py
@@ -148,23 +148,14 @@
     pairs = n_col // 2
     own_slot = col % 2 * pairs + col // 2
     slot = pl.ds(pl.multiple_of(corners + own_slot * sel, sel), sel)
+    other_slot = (1 - col % 2) * pairs + col // 2
+    partner_slot = pl.ds(pl.multiple_of(corners + other_slot * sel, sel), sel)
     parity_slots = pl.ds(pl.multiple_of(corners + col % 2 * pairs * sel, sel), pairs * sel)
 
     loads[0].wait()
     loads[1].wait()
     for t in range(2):
         halves[t] = jnp.dot(split_order, own_kv[t], preferred_element_type=F32).astype(BF16)
-    pl.semaphore_wait(
-        barrier,
-        len(same_parity)
-        + jnp.where(has_up, 1, 0) + jnp.where(has_down, 1, 0)
-        + jnp.where(has_left, 1, 0) + jnp.where(has_right, 1, 0),
-    )
-    for t in range(2):
-        pl.when(has_left)(to_left[t].start)
-        pl.when(has_right)(to_right[t].start)
-    pl.when(has_up)(to_up.start)
-    pl.when(has_down)(to_down.start)
     for t in range(2):
         by_phase = jnp.dot(phase_order, own_kv[t], preferred_element_type=F32)
         picked = jnp.zeros((sel, width), F32)
@@ -173,20 +164,37 @@
         picked = picked.astype(BF16)
         chosen[t] = picked
         far_kv[t, slot] = picked
-    dil = []
-    for d, peer in enumerate(same_parity):
-        copy = pltpu.make_async_remote_copy(
-            src_ref=chosen, dst_ref=far_kv.at[:, slot],
-            send_sem=dil_send.at[d], recv_sem=dil_recv.at[d],
-            device_id=peer, device_id_type=MESH,
+    pl.semaphore_wait(
+        barrier,
+        len(same_parity)
+        + jnp.where(has_up, 1, 0) + jnp.where(has_down, 1, 0)
+        + jnp.where(has_left, 1, 0) + jnp.where(has_right, 1, 0),
+    )
+    def dil_copy(t, src, rows, sem, device):
+        return pltpu.make_async_remote_copy(
+            src_ref=src, dst_ref=far_kv.at[t, rows],
+            send_sem=dil_send.at[sem], recv_sem=dil_recv.at[sem],
+            device_id=device, device_id_type=MESH,
         )
+
+    key_spread = [dil_copy(0, chosen.at[0], slot, d, p) for d, p in enumerate(same_parity)]
+    value_spread = [
+        dil_copy(1, chosen.at[1], slot, pairs + d, p) for d, p in enumerate(same_parity)
+    ]
+    value_swap = dil_copy(1, chosen.at[1], slot, 2 * pairs, partner)
+    value_relay = [
+        dil_copy(1, far_kv.at[1, partner_slot], partner_slot, 2 * pairs + 1 + d, p)
+        for d, p in enumerate(same_parity)
+    ]
+    key_swap = dil_copy(0, far_kv.at[0, parity_slots], parity_slots, 3 * pairs + 1, partner)
+    value_swap.start()
+    for t in range(2):
+        pl.when(has_left)(to_left[t].start)
+        pl.when(has_right)(to_right[t].start)
+    pl.when(has_up)(to_up.start)
+    pl.when(has_down)(to_down.start)
+    for copy in key_spread + value_spread:
         copy.start()
-        dil.append(copy)
-    to_partner = pltpu.make_async_remote_copy(
-        src_ref=far_kv.at[:, parity_slots], dst_ref=far_kv.at[:, parity_slots],
-        send_sem=dil_send.at[pairs], recv_sem=dil_recv.at[pairs],
-        device_id=partner, device_id_type=MESH,
-    )
 
     def clear(ref, first, count):
         ref[:, pl.ds(first, count)] = jnp.zeros((2, count, width), BF16)
@@ -262,6 +270,9 @@
                     highest[head], total[head], numer[head] = top, new_total, new_numer
         return finished
 
+    value_swap.wait_recv()
+    for copy in value_relay:
+        copy.start()
     attend(own_kv, 0, tiles, lambda head: bias_own[...], True, False)
 
     for block, shift in ((0, -dr), (1, dr)):
@@ -312,14 +323,15 @@
             pl.when(has_up)(right_to_up[t].start)
             pl.when(has_down)(right_to_down[t].start)
 
-    for copy in dil:
+    for copy in key_spread:
         copy.wait_recv()
-    to_partner.start()
+    key_swap.start()
 
     attend(
         mid_kv, 2 * tiles, tiles, lambda head: bias_mid[pl.ds(2 * tiles, tiles)], False, False
     )
-    to_partner.wait_recv()
+    for copy in [key_swap] + value_spread + value_relay:
+        copy.wait_recv()
     for t in range(2):
         pl.when(has_left & has_up)(left_to_down[t].wait_recv)
         pl.when(has_left & has_down)(left_to_up[t].wait_recv)
@@ -340,9 +352,8 @@
         pl.when(has_left & has_down)(left_to_down[t].wait_send)
         pl.when(has_right & has_up)(right_to_up[t].wait_send)
         pl.when(has_right & has_down)(right_to_down[t].wait_send)
-    for copy in dil:
+    for copy in key_spread + value_spread + value_relay + [value_swap, key_swap]:
         copy.wait_send()
-    to_partner.wait_send()
 
 
 def solution(mesh):
@@ -378,8 +389,8 @@
                 pltpu.SemaphoreType.DMA((3,)),
                 pltpu.SemaphoreType.DMA((14,)),
                 pltpu.SemaphoreType.DMA((14,)),
-                pltpu.SemaphoreType.DMA((n_col,)),
-                pltpu.SemaphoreType.DMA((n_col,)),
+                pltpu.SemaphoreType.DMA((2 * n_col,)),
+                pltpu.SemaphoreType.DMA((2 * n_col,)),
             ],
             compiler_params=pltpu.CompilerParams(
                 collective_id=0, has_side_effects=True, vmem_limit_bytes=56 * 1024 * 1024

time: 27.2 us -> 27.1 us (level)
  the two profiles are of different devices: /device:TPU:0 before, /device:TPU:9 now
where the time goes in v6:
time: 27.1 us; the launch traced here: 26.9 us
  Pallas kernels  24.9 us (92%)
  matrix products  1.93 us (7%)
    pallas_call x1, Pallas kernels, per_device(): pl.pallas_call(functools.partial(kernel, n_row, n_col, dr, dc), out_shape...  24.9 us
    dot_general x1, matrix products, per_device(): jnp.dot(out, output_matrix, preferred_element_type=F32).astype(BF16)  1.93 us

profile of v6, /device:TPU:9, one launch (start us, length us, event | category | flops | bytes accessed | tf_op | source)
XLA Modules:
  0.0 26.9 jit_solution(13610586566310542047)
XLA Ops:
  0.0 0.0 copy-start
  0.0 24.9 %shard_map.73 = bf16[128,768]{1,0:T(8,128)(2,1)} custom-call(bf16[128,768]{1,0:T(8,128)(2,1)} %bitcast.6, bf16[128,768]{1,0:T(8,128)(2,1)} %bitcast.7, bf16[128,768]{1,0:T(8,128)(2,1)} %bitcast.8, s32[32,128]{1,0:T(8,128)} %tissue_ref.1, s32[16]{0:T(128)} %dil_ref.1, s32[16]{0:T(128)} %seg_ref.1), custom_call_target="tpu_custom_call" | custom-call | tf_op jit(solution)/shard_map/pallas_call | solution.py:370
  24.9 0.0 copy-done
  25.0 1.9 %convolution_convert_fusion = bf16[128,768]{1,0:T(8,128)(2,1)} fusion(bf16[128,768]{1,0:T(8,128)(2,1)} %shard_map.73, bf16[768,768]{1,0:T(8,128)(2,1)S(1)} %copy-done), kind=kOutput, calls=%fused_computation | convolution fusion | flops 151093248 | bytes 1572864 | tf_op jit(solution)/shard_map/dot_general | solution.py:402
Async XLA Ops:
  0.0 24.9 %copy-start = (bf16[768,768]{1,0:T(8,128)(2,1)S(1)}, bf16[768,768]{1,0:T(8,128)(2,1)}, u32[]{:S(2)}) copy-start(bf16[768,768]{1,0:T(8,128)(2,1)} %param.13) | copy-start | bytes 3538948

commit v7 on v6

--- a/solution.py
+++ b/solution.py
@@ -84,6 +84,7 @@
 
     has_up, has_down = row > 0, row < n_row - 1
     has_left, has_right = col > 0, col < n_col - 1
+    even, odd = row % 2 == 0, row % 2 == 1
     up = (lax.rem(row + n_row - 1, n_row), col)
     down = (lax.rem(row + 1, n_row), col)
     left = (row, lax.rem(col + n_col - 1, n_col))
@@ -191,8 +192,11 @@
     for t in range(2):
         pl.when(has_left)(to_left[t].start)
         pl.when(has_right)(to_right[t].start)
-    pl.when(has_up)(to_up.start)
-    pl.when(has_down)(to_down.start)
+        if t == 0:
+            pl.when(has_up & even)(to_up.start)
+            pl.when(has_down & odd)(to_down.start)
+    pl.when(has_up & odd)(to_up.start)
+    pl.when(has_down & even)(to_down.start)
     for copy in key_spread + value_spread:
         copy.start()
 
@@ -310,18 +314,14 @@
     attend(mid_kv, 0, 2 * tiles, lambda head: bias_mid[pl.ds(0, 2 * tiles)], False, False)
 
     for t in range(2):
-
-        @pl.when(has_left)
-        def _(t=t):
-            to_right[t].wait_recv()
-            pl.when(has_up)(left_to_up[t].start)
-            pl.when(has_down)(left_to_down[t].start)
-
-        @pl.when(has_right)
-        def _(t=t):
-            to_left[t].wait_recv()
-            pl.when(has_up)(right_to_up[t].start)
-            pl.when(has_down)(right_to_down[t].start)
+        for have, arrived, upward, downward in (
+            (has_left, to_right[t], left_to_up[t], left_to_down[t]),
+            (has_right, to_left[t], right_to_up[t], right_to_down[t]),
+        ):
+            pl.when(have)(arrived.wait_recv)
+            pl.when(have & has_up & even)(upward.start)
+            pl.when(have & has_down)(downward.start)
+            pl.when(have & has_up & odd)(upward.start)
 
     for copy in key_spread:
         copy.wait_recv()
@@ -330,17 +330,25 @@
     attend(
         mid_kv, 2 * tiles, tiles, lambda head: bias_mid[pl.ds(2 * tiles, tiles)], False, False
     )
+    def corners_arrived(from_up, from_down):
+        for t in range(2):
+            pl.when(has_left & has_up & from_up)(left_to_down[t].wait_recv)
+            pl.when(has_right & has_up & from_up)(right_to_down[t].wait_recv)
+            pl.when(has_left & has_down & from_down)(left_to_up[t].wait_recv)
+            pl.when(has_right & has_down & from_down)(right_to_up[t].wait_recv)
+
+    def far_stage(begin, count, last):
+        return attend(
+            far_kv, begin, count, lambda head: bias_far[head, pl.ds(begin, count)], False, last
+        )
+
+    corners_arrived(odd, even)
+    far_stage(pl.multiple_of((1 - row % 2) * tiles, tiles), tiles, False)
     for copy in [key_swap] + value_spread + value_relay:
         copy.wait_recv()
-    for t in range(2):
-        pl.when(has_left & has_up)(left_to_down[t].wait_recv)
-        pl.when(has_left & has_down)(left_to_up[t].wait_recv)
-        pl.when(has_right & has_up)(right_to_down[t].wait_recv)
-        pl.when(has_right & has_down)(right_to_up[t].wait_recv)
-
-    finished = attend(
-        far_kv, 0, corners + n_dil, lambda head: bias_far[head], False, True
-    )
+    far_stage(corners, n_dil, False)
+    corners_arrived(even, odd)
+    finished = far_stage(pl.multiple_of(row % 2 * tiles, tiles), tiles, True)
     out_ref[...] = jnp.concatenate(finished, axis=0).T.astype(BF16)
 
     pl.when(has_up)(to_up.wait_send)

time: 27.1 us -> 26.5 us (0.978)
  the two profiles are of different devices: /device:TPU:9 before, /device:TPU:0 now
where the time goes in v7:
time: 26.5 us; the launch traced here: 26.3 us
  Pallas kernels  24.4 us (92%)
  matrix products  1.93 us (7%)
    pallas_call x1, Pallas kernels, per_device(): pl.pallas_call(functools.partial(kernel, n_row, n_col, dr, dc), out_shape...  24.4 us
    dot_general x1, matrix products, per_device(): jnp.dot(out, output_matrix, preferred_element_type=F32).astype(BF16)  1.93 us

profile of v7, /device:TPU:0, one launch (start us, length us, event | category | flops | bytes accessed | tf_op | source)
XLA Modules:
  0.0 26.3 jit_solution(13076900816573799222)
XLA Ops:
  0.0 0.0 copy-start
  0.0 24.4 %shard_map.73 = bf16[128,768]{1,0:T(8,128)(2,1)} custom-call(bf16[128,768]{1,0:T(8,128)(2,1)} %bitcast.6, bf16[128,768]{1,0:T(8,128)(2,1)} %bitcast.7, bf16[128,768]{1,0:T(8,128)(2,1)} %bitcast.8, s32[32,128]{1,0:T(8,128)} %tissue_ref.1, s32[16]{0:T(128)} %dil_ref.1, s32[16]{0:T(128)} %seg_ref.1), custom_call_target="tpu_custom_call" | custom-call | tf_op jit(solution)/shard_map/pallas_call | solution.py:378
  24.4 0.0 copy-done
  24.4 1.9 %convolution_convert_fusion = bf16[128,768]{1,0:T(8,128)(2,1)} fusion(bf16[128,768]{1,0:T(8,128)(2,1)} %shard_map.73, bf16[768,768]{1,0:T(8,128)(2,1)S(1)} %copy-done), kind=kOutput, calls=%fused_computation | convolution fusion | flops 151093248 | bytes 1572864 | tf_op jit(solution)/shard_map/dot_general | solution.py:410
Async XLA Ops:
  0.0 24.4 %copy-start = (bf16[768,768]{1,0:T(8,128)(2,1)S(1)}, bf16[768,768]{1,0:T(8,128)(2,1)}, u32[]{:S(2)}) copy-start(bf16[768,768]{1,0:T(8,128)(2,1)} %param.13) | copy-start | bytes 3538948

commit v8 on v7

--- a/solution.py
+++ b/solution.py
@@ -127,13 +127,16 @@
     to_left, to_right, left_to_up, left_to_down, right_to_up, right_to_down = (
         [], [], [], [], [], []
     )
-    for t in range(2):
-        left_here = mid_kv.at[t, pl.ds(2 * tiles, half)]
-        right_here = mid_kv.at[t, pl.ds(2 * tiles + half, half)]
-        corner = [far_kv.at[t, pl.ds(index * half, half)] for index in range(4)]
-        sem = 2 + 6 * t
-        to_left.append(remote(halves.at[t, pl.ds(0, half)], right_here, sem, left))
-        to_right.append(remote(halves.at[t, pl.ds(half, half)], left_here, sem + 1, right))
+    piece = half // 2
+    pieces = range(4)
+    for n in pieces:
+        t, skip = n // 2, n % 2 * piece
+        left_here = mid_kv.at[t, pl.ds(2 * tiles + skip, piece)]
+        right_here = mid_kv.at[t, pl.ds(2 * tiles + half + skip, piece)]
+        corner = [far_kv.at[t, pl.ds(index * half + skip, piece)] for index in range(4)]
+        sem = 2 + 6 * n
+        to_left.append(remote(halves.at[t, pl.ds(skip, piece)], right_here, sem, left))
+        to_right.append(remote(halves.at[t, pl.ds(half + skip, piece)], left_here, sem + 1, right))
         left_to_up.append(remote(left_here, corner[2], sem + 2, up))
         left_to_down.append(remote(left_here, corner[0], sem + 3, down))
         right_to_up.append(remote(right_here, corner[3], sem + 4, up))
@@ -189,10 +192,10 @@
     ]
     key_swap = dil_copy(0, far_kv.at[0, parity_slots], parity_slots, 3 * pairs + 1, partner)
     value_swap.start()
-    for t in range(2):
+    for t in pieces:
         pl.when(has_left)(to_left[t].start)
         pl.when(has_right)(to_right[t].start)
-        if t == 0:
+        if t == 1:
             pl.when(has_up & even)(to_up.start)
             pl.when(has_down & odd)(to_down.start)
     pl.when(has_up & odd)(to_up.start)
@@ -242,9 +245,8 @@
                 head_mask(g, h, hd), lanes, jnp.zeros_like(lanes)
             )
 
-    def attend(kv, begin, count, extra, first, last):
+    def attend(kv, begin, count, extra, first):
         values = kv[1, pl.ds(begin, count)].T
-        finished = []
         for g in range(groups):
             base, _ = lane_window(g, hd)
             scores = lax.dot_general(
@@ -268,16 +270,12 @@
                     keep = jnp.exp2((old_top - top) * factor)
                     new_total += keep * total[head]
                     new_numer += keep * numer[head]
-                if last:
-                    finished.append(new_numer * (1.0 / new_total))
-                else:
-                    highest[head], total[head], numer[head] = top, new_total, new_numer
-        return finished
+                highest[head], total[head], numer[head] = top, new_total, new_numer
 
     value_swap.wait_recv()
     for copy in value_relay:
         copy.start()
-    attend(own_kv, 0, tiles, lambda head: bias_own[...], True, False)
+    attend(own_kv, 0, tiles, lambda head: bias_own[...], True)
 
     for block, shift in ((0, -dr), (1, dr)):
         shared = bias(tiles, lambda k: k % half // R + shift, half_col)
@@ -311,9 +309,9 @@
 
     pl.when(has_down)(to_up.wait_recv)
     pl.when(has_up)(to_down.wait_recv)
-    attend(mid_kv, 0, 2 * tiles, lambda head: bias_mid[pl.ds(0, 2 * tiles)], False, False)
-
-    for t in range(2):
+    attend(mid_kv, 0, 2 * tiles, lambda head: bias_mid[pl.ds(0, 2 * tiles)], False)
+
+    for t in pieces:
         for have, arrived, upward, downward in (
             (has_left, to_right[t], left_to_up[t], left_to_down[t]),
             (has_right, to_left[t], right_to_up[t], right_to_down[t]),
@@ -328,32 +326,35 @@
     key_swap.start()
 
     attend(
-        mid_kv, 2 * tiles, tiles, lambda head: bias_mid[pl.ds(2 * tiles, tiles)], False, False
+        mid_kv, 2 * tiles, tiles, lambda head: bias_mid[pl.ds(2 * tiles, tiles)], False
     )
     def corners_arrived(from_up, from_down):
-        for t in range(2):
+        for t in pieces:
             pl.when(has_left & has_up & from_up)(left_to_down[t].wait_recv)
             pl.when(has_right & has_up & from_up)(right_to_down[t].wait_recv)
             pl.when(has_left & has_down & from_down)(left_to_up[t].wait_recv)
             pl.when(has_right & has_down & from_down)(right_to_up[t].wait_recv)
 
-    def far_stage(begin, count, last):
-        return attend(
-            far_kv, begin, count, lambda head: bias_far[head, pl.ds(begin, count)], False, last
-        )
+    def far_stage(begin, count):
+        attend(far_kv, begin, count, lambda head: bias_far[head, pl.ds(begin, count)], False)
 
     corners_arrived(odd, even)
-    far_stage(pl.multiple_of((1 - row % 2) * tiles, tiles), tiles, False)
+    far_stage(pl.multiple_of((1 - row % 2) * tiles, tiles), tiles)
     for copy in [key_swap] + value_spread + value_relay:
         copy.wait_recv()
-    far_stage(corners, n_dil, False)
+    far_stage(corners, n_dil)
     corners_arrived(even, odd)
-    finished = far_stage(pl.multiple_of(row % 2 * tiles, tiles), tiles, True)
+
+    @pl.when((has_up & even) | (has_down & odd))
+    def _():
+        far_stage(pl.multiple_of(row % 2 * tiles, tiles), tiles)
+
+    finished = [numer[head] * (1.0 / total[head]) for head in range(HEAD_COUNT)]
     out_ref[...] = jnp.concatenate(finished, axis=0).T.astype(BF16)
 
     pl.when(has_up)(to_up.wait_send)
     pl.when(has_down)(to_down.wait_send)
-    for t in range(2):
+    for t in pieces:
         pl.when(has_left)(to_left[t].wait_send)
         pl.when(has_right)(to_right[t].wait_send)
         pl.when(has_left & has_up)(left_to_up[t].wait_send)
@@ -395,8 +396,8 @@
                 pltpu.VMEM((HEAD_COUNT, 1, tiles), F32),
                 pltpu.VMEM((HEAD_COUNT, 1, tiles), F32),
                 pltpu.SemaphoreType.DMA((3,)),
-                pltpu.SemaphoreType.DMA((14,)),
-                pltpu.SemaphoreType.DMA((14,)),
+                pltpu.SemaphoreType.DMA((26,)),
+                pltpu.SemaphoreType.DMA((26,)),
                 pltpu.SemaphoreType.DMA((2 * n_col,)),
                 pltpu.SemaphoreType.DMA((2 * n_col,)),
             ],

time: 26.5 us -> 26.7 us (level)
  the two profiles are of different devices: /device:TPU:0 before, /device:TPU:9 now
where the time goes in v8:
time: 26.7 us; the launch traced here: 26.5 us
  Pallas kernels  24.6 us (92%)
  matrix products  1.93 us (7%)
    pallas_call x1, Pallas kernels, per_device(): pl.pallas_call(functools.partial(kernel, n_row, n_col, dr, dc), out_shape...  24.6 us
    dot_general x1, matrix products, per_device(): jnp.dot(out, output_matrix, preferred_element_type=F32).astype(BF16)  1.93 us

profile of v8, /device:TPU:9, one launch (start us, length us, event | category | flops | bytes accessed | tf_op | source)
XLA Modules:
  0.0 26.5 jit_solution(17286522717670340423)
XLA Ops:
  0.0 0.0 copy-start
  0.0 24.6 %shard_map.73 = bf16[128,768]{1,0:T(8,128)(2,1)} custom-call(bf16[128,768]{1,0:T(8,128)(2,1)} %bitcast.6, bf16[128,768]{1,0:T(8,128)(2,1)} %bitcast.7, bf16[128,768]{1,0:T(8,128)(2,1)} %bitcast.8, s32[32,128]{1,0:T(8,128)} %tissue_ref.1, s32[16]{0:T(128)} %dil_ref.1, s32[16]{0:T(128)} %seg_ref.1), custom_call_target="tpu_custom_call" | custom-call | tf_op jit(solution)/shard_map/pallas_call | solution.py:379
  24.6 0.0 copy-done
  24.6 1.9 %convolution_convert_fusion = bf16[128,768]{1,0:T(8,128)(2,1)} fusion(bf16[128,768]{1,0:T(8,128)(2,1)} %shard_map.73, bf16[768,768]{1,0:T(8,128)(2,1)S(1)} %copy-done), kind=kOutput, calls=%fused_computation | convolution fusion | flops 151093248 | bytes 1572864 | tf_op jit(solution)/shard_map/dot_general | solution.py:411
Async XLA Ops:
  0.0 24.6 %copy-start = (bf16[768,768]{1,0:T(8,128)(2,1)S(1)}, bf16[768,768]{1,0:T(8,128)(2,1)}, u32[]{:S(2)}) copy-start(bf16[768,768]{1,0:T(8,128)(2,1)} %param.13) | copy-start | bytes 3538948
